TPU v7x, 128 devices: a whole 4x4x4 slice. The times are simulated.
128 devices in a mesh: ctx: 16 (over y, x), tp: 8 (over z, core).
Axes of the slice: x: 4, y: 4, z: 4, core: 2. Of those that a mesh axis runs over, the one named last changes fastest.
Arguments:
- tokens_in: bfloat16 [4096, 8192], P('ctx', 'tp'), may hold values from -6 to 6
- base_queries: bfloat16 [4096, 8192], P('ctx', 'tp'), may hold values from -6 to 6
- fresh_keys: bfloat16 [4096, 1024], P('ctx', 'tp'), may hold values from -6 to 6
- fresh_values: bfloat16 [4096, 1024], P('ctx', 'tp'), may hold values from -6 to 6
- cached_key_rows: bfloat16 [16384, 1024], P('ctx', 'tp'), may hold values from -6 to 6
- cached_value_rows: bfloat16 [16384, 1024], P('ctx', 'tp'), may hold values from -6 to 6
- adapter_store: bfloat16 [64, 2, 64, 8192], P('ctx', None, None, 'tp'), may hold values from -0.125 to 0.125
- adapter_slot: int32 [64], replicated, may hold values from 0 to 63, each once
- segment_adapter: int32 [17], replicated, may hold values from 0 to 63
- token_request: int32 [4096], P('ctx'), may hold values from 0 to 16, as said below
- cache_doc: int32 [128], P('ctx'), may hold values from 0 to 16
Outputs:
- attended: bfloat16 [4096, 8192], P('ctx', 'tp')
Inputs may be any that keep to these rules, and one draw needn't show every extreme that they name: `token_request`: segment ids never fall; each aligned block of 256 tokens begins inside the segment that began in the block before (the first block with segment 0) and starts exactly one new segment, at a position of 1 to 254 of the block.
All inputs are finite; a program needn't handle non-finite values.
Results may differ from a plain program's by a relative error of at most 0.024.
Values may be sent and summed in bfloat16 or wider, within the bound.
No kernel may reach another device: no remote copies, remote signals or barrier semaphores. Data moves between devices by JAX's collectives and lax.ppermute only.
A program may use at most 128 MiB of HBM per device.

v0:
```python
import math

import jax
import jax.numpy as jnp
from jax import lax
from jax.sharding import PartitionSpec as P

HEAD_SIZE = 128
PAGE = 128


adapter_scale = 2.0


def shifted(block, axis, distance):
    devices = range(lax.axis_size(axis))
    route = [(i - distance, i) for i in devices if i - distance in devices]
    return lax.ppermute(block, axis, route)


def update_softmax(carry_state, query_rows, key_matrix, value_matrix, visible, score_scale):
    run_max, run_sum, run_out = carry_state
    count_rows = key_matrix.shape[0]
    kv_local = query_rows.shape[1]
    key_three = key_matrix.reshape(count_rows, kv_local, -1)
    value_three = value_matrix.reshape(count_rows, kv_local, -1)
    scores = (
        jnp.einsum("tkgd,nkd->tkgn", query_rows, key_three, preferred_element_type=jnp.float32)
        * score_scale
    )
    wide_mask = visible[:, None, None, :]
    peak = jnp.max(jnp.where(wide_mask, scores, -1e30), axis=-1)
    new_max = jnp.maximum(run_max, peak)
    weights = jnp.where(wide_mask, jnp.exp(scores - new_max[..., None]), 0.0)
    fading = jnp.exp(run_max - new_max)
    run_sum = run_sum * fading + jnp.sum(weights, axis=-1)
    added = jnp.einsum(
        "tkgn,nkd->tkgd",
        weights.astype(jnp.bfloat16),
        value_three,
        preferred_element_type=jnp.float32,
    )
    run_out = run_out * fading[..., None] + added
    return (new_max, run_sum, run_out)


def per_device(
    tokens_in,
    base_queries,
    fresh_keys,
    fresh_values,
    cached_key_rows,
    cached_value_rows,
    adapter_store,
    adapter_slot,
    segment_adapter,
    token_request,
    cache_doc,
):
    tok_rows = tokens_in.shape[0]
    per_owner = adapter_store.shape[0]
    rank_size = adapter_store.shape[2]
    feature_cols = adapter_store.shape[3]
    first_segment = token_request[0]
    slot_index = token_request - first_segment
    needed = adapter_slot[segment_adapter[first_segment + jnp.arange(2, dtype=jnp.int32)]]
    flat_store = adapter_store.reshape(per_owner, -1)
    piece = lax.all_gather(flat_store, "ctx", axis=0, tiled=True)
    row_index = jnp.arange(piece.shape[0], dtype=jnp.int32)
    selector = (needed[:, None] == row_index[None, :]).astype(jnp.bfloat16)
    gathered = jnp.dot(selector, piece, preferred_element_type=jnp.float32)
    blocks = gathered.astype(jnp.bfloat16).reshape(2, 2, rank_size, feature_cols)
    down_rank = blocks[:, 0]
    up_rank = blocks[:, 1]
    rank_acts = jnp.einsum("td,srd->tsr", tokens_in, down_rank, preferred_element_type=jnp.float32)
    rank_acts = lax.psum(
        rank_acts.reshape(tok_rows, 2 * rank_size).astype(jnp.bfloat16), "tp"
    ).astype(jnp.float32)
    rank_acts = rank_acts.reshape(tok_rows, 2, rank_size)
    chosen = slot_index[:, None, None] == jnp.arange(2, dtype=jnp.int32)[None, :, None]
    rank_round = (
        jnp.where(chosen, rank_acts, 0.0).astype(jnp.bfloat16).reshape(tok_rows, 2 * rank_size)
    )
    adapter_term = jnp.dot(
        rank_round, up_rank.reshape(2 * rank_size, feature_cols), preferred_element_type=jnp.float32
    )
    query_rows = (base_queries.astype(jnp.float32) + adapter_scale * adapter_term).astype(
        jnp.bfloat16
    )
    kv_local = fresh_keys.shape[1] // HEAD_SIZE
    group_width = query_rows.shape[1] // HEAD_SIZE // kv_local
    query_rows = query_rows.reshape(tok_rows, kv_local, group_width, HEAD_SIZE)
    score_scale = 1.0 / math.sqrt(HEAD_SIZE)
    prev_keys, prev_values, prev_segment = shifted(
        (fresh_keys, fresh_values, (token_request + 1).astype(jnp.bfloat16)), "ctx", 1
    )
    span_keys = jnp.concatenate([prev_keys, fresh_keys], axis=0)
    span_values = jnp.concatenate([prev_values, fresh_values], axis=0)
    span_segment = jnp.concatenate([prev_segment.astype(jnp.int32) - 1, token_request])
    span_place = jnp.arange(2 * tok_rows, dtype=jnp.int32) - tok_rows
    query_place = jnp.arange(tok_rows, dtype=jnp.int32)
    visible = (span_segment[None, :] == token_request[:, None]) & (
        span_place[None, :] <= query_place[:, None]
    )
    start_state = (
        jnp.full((tok_rows, kv_local, group_width), -1e30, jnp.float32),
        jnp.zeros((tok_rows, kv_local, group_width), jnp.float32),
        jnp.zeros((tok_rows, kv_local, group_width, HEAD_SIZE), jnp.float32),
    )
    carry_state = update_softmax(
        start_state, query_rows, span_keys, span_values, visible, score_scale
    )
    doc_rows = jnp.repeat(cache_doc, PAGE).astype(jnp.bfloat16)
    key_matrix = lax.all_gather(cached_key_rows, "ctx", axis=0, tiled=True)
    value_matrix = lax.all_gather(cached_value_rows, "ctx", axis=0, tiled=True)
    doc_piece = lax.all_gather(doc_rows, "ctx", axis=0, tiled=True)
    count_rows = key_matrix.shape[0]
    block_rows = 1024
    steps_count = count_rows // block_rows

    def scan_block(state_now, block_part):
        key_part, value_part, doc_part = block_part
        seen = doc_part.astype(jnp.int32)[None, :] == token_request[:, None]
        return (
            update_softmax(state_now, query_rows, key_part, value_part, seen, score_scale),
            None,
        )

    state_out, unused = lax.scan(
        scan_block,
        carry_state,
        (
            key_matrix.reshape(steps_count, block_rows, -1),
            value_matrix.reshape(steps_count, block_rows, -1),
            doc_piece.reshape(steps_count, block_rows),
        ),
    )
    run_max, run_sum, run_out = state_out
    attended = run_out / run_sum[..., None]
    return attended.reshape(tok_rows, kv_local * group_width * HEAD_SIZE).astype(jnp.bfloat16)


def solution(mesh):
    in_specs = (
        P("ctx", "tp"),
        P("ctx", "tp"),
        P("ctx", "tp"),
        P("ctx", "tp"),
        P("ctx", "tp"),
        P("ctx", "tp"),
        P("ctx", None, None, "tp"),
        P(),
        P(),
        P("ctx"),
        P("ctx"),
    )
    out_specs = P("ctx", "tp")
    return jax.shard_map(
        per_device, mesh=mesh, in_specs=in_specs, out_specs=out_specs, check_vma=False
    )
```

profile of v0, /device:TPU:22, one launch (start us, length us, event | category | flops | bytes accessed | tf_op | source)
XLA Modules:
  0.0 435.7 jit_solution(18426165798346884461)
XLA Ops:
  6.5 3.0 reshape.284
  9.6 1.2 slice.9
  11.5 1.3 gather_fusion
  12.8 1.3 gather_fusion.1
  14.1 107.4 %all-gather.9.cloned.1.call-done = bf16[16,4,131072]{2,1,0:T(4,128)(2,1)} async-done(((bf16[1,4,131072]{2,1,0:T(4,128)(2,1)}), bf16[16,4,131072]{2,1,0:T(4,128)(2,1)}) %all-gather.9.cloned.1.call-update) | async-done | bytes 16777232 | tf_op jit(solution)/shard_map/all_gather | solution.py:68
  121.5 15.0 %reshape.285 = bf16[64,131072]{1,0:T(8,128)(2,1)} reshape(bf16[16,4,131072]{2,1,0:T(4,128)(2,1)} %all-gather.9.cloned.1.call-done) | data formatting | bytes 33554432
  136.6 8.2 %convolution_convert_fusion = bf16[2,131072]{1,0:T(2,128)(2,1)S(1)} fusion(bf16[64,131072]{1,0:T(8,128)(2,1)} %reshape.285, s32[2]{0:T(128)S(1)} %gather_fusion.1), kind=kOutput, calls=%fused_computation.30 | convolution fusion | flops 33816704 | bytes 17301512 | tf_op jit(solution)/shard_map/dot_general | solution.py:71
  147.8 4.6 %collective-permute-start = (bf16[256]{0:T(256)(128)(2,1)S(1)}, bf16[256]{0:T(256)(128)(2,1)S(1)}, u32[]{:S(2)}, u32[]{:S(2)}) collective-permute-start(bf16[256]{0:T(256)(128)(2,1)S(1)} %get-tuple-element.107), channel_id=1, source_target_pairs={{0,8},{8,16},{16,24},{24,32},{32,40},{40,48},{48,56},{56,64},{64,7... | collective-permute-start | bytes 1544 | tf_op jit(solution)/shard_map/ppermute | solution.py:18
  152.4 2.2 collective-permute-start.1
  154.7 3.1 collective-permute-start.2
  157.9 21.3 %all_gather.13 = bf16[16384]{0:T(1024)(128)(2,1)S(1)} all-gather(bf16[1024]{0:T(1024)(128)(2,1)S(1)} %broadcast_bitcast_fusion), channel_id=1, replica_groups=mesh['ctx'=16,'tp'=8] {'ctx'}, dimensions={0}, use_global_device_ids=true | all-gather | bytes 34816 | tf_op jit(solution)/shard_map/all_gather | solution.py:116
  179.5 26.8 %all-reduce.2.cloned.1.call-done = bf16[256,128]{0,1:T(8,128)(2,1)} async-done(((bf16[256,128]{0,1:T(8,128)(2,1)}), bf16[256,128]{0,1:T(8,128)(2,1)}) %all-reduce.2.cloned.1.call-update) | async-done | bytes 65552 | tf_op jit(solution)/shard_map/psum | solution.py:76
  209.3 1.0 fusion.42
  210.3 47.0 %all-gather.5.cloned.1.call-done = bf16[16384,128]{1,0:T(8,128)(2,1)} async-done(((bf16[1024,128]{1,0:T(8,128)(2,1)}), bf16[16384,128]{1,0:T(8,128)(2,1)}) %all-gather.5.cloned.1.call-update) | async-done | bytes 4194320 | tf_op jit(solution)/shard_map/all_gather | solution.py:114
  257.3 53.4 %all-gather.7.cloned.1.call-done = bf16[16384,128]{1,0:T(8,128)(2,1)} async-done(((bf16[1024,128]{1,0:T(8,128)(2,1)}), bf16[16384,128]{1,0:T(8,128)(2,1)}) %all-gather.7.cloned.1.call-update) | async-done | bytes 4194320 | tf_op jit(solution)/shard_map/all_gather | solution.py:115
  310.7 117.3 %while.14 = (s32[]{:T(128)}, f32[256,1,8]{0,2,1:T(8,128)S(1)}, f32[256,1,8]{0,2,1:T(8,128)S(1)}, f32[256,1,8,128]{0,3,2,1:T(8,128)S(1)}, bf16[16,1024]{1,0:T(8,1...) while((s32[]{:T(128)}, f32[256,1,8]{0,2,1:T(8,128)S(1)}, ...), condition=%wide.region_6.7_spmd, body=%wide.region_3.6_spmd.sunk | while | flops 1097604096 | bytes 29503592 | solution.py:129
  310.9 2.3 fusion.77
  313.3 3.0 fusion.80
  316.2 1.7 fusion.79
  318.2 2.3 fusion.77
  320.6 3.0 fusion.80
  323.6 1.7 fusion.79
  325.6 2.3 fusion.77
  327.9 3.0 fusion.80
  330.9 1.7 fusion.79
  332.9 2.3 fusion.77
  335.3 3.0 fusion.80
  338.2 1.7 fusion.79
  340.2 2.3 fusion.77
  342.6 3.0 fusion.80
  345.6 1.7 fusion.79
  347.6 2.3 fusion.77
  349.9 3.0 fusion.80
  352.9 1.7 fusion.79
  354.9 2.3 fusion.77
  357.3 3.0 fusion.80
  360.2 1.7 fusion.79
  362.2 2.3 fusion.77
  364.6 3.0 fusion.80
  367.6 1.7 fusion.79
  369.6 2.3 fusion.77
  371.9 3.0 fusion.80
  374.9 1.7 fusion.79
  376.9 2.3 fusion.77
  379.3 3.0 fusion.80
  382.3 1.7 fusion.79
  384.2 2.3 fusion.77
  386.6 3.0 fusion.80
  389.6 1.7 fusion.79
  391.6 2.3 fusion.77
  393.9 3.0 fusion.80
  396.9 1.7 fusion.79
  398.9 2.3 fusion.77
  401.3 3.0 fusion.80
  404.3 1.7 fusion.79
  406.3 2.3 fusion.77
  408.6 3.0 fusion.80
  411.6 1.7 fusion.79
  413.6 2.3 fusion.77
  416.0 3.0 fusion.80
  418.9 1.7 fusion.79
  420.9 2.3 fusion.77
  423.3 3.0 fusion.80
  426.3 1.7 fusion.79
  (130 shorter events, 12.3 us)
Async XLA Ops:
  6.5 138.3 %copy-start = (bf16[256,1024]{1,0:T(8,128)(2,1)S(1)}, bf16[256,1024]{1,0:T(8,128)(2,1)}, u32[]{:S(2)}) copy-start(bf16[256,1024]{1,0:T(8,128)(2,1)} %param.13) | copy-start | bytes 1572868
  6.5 115.0 %all-gather.9.cloned.1.call-start = ((), (), s32[]{:S(2)}) async-start(), calls=%async_computation.3 | async-start | bytes 17825792 | tf_op jit(solution)/shard_map/all_gather | solution.py:68
  9.6 196.6 %all-reduce.2.cloned.1.call-start = ((), (), s32[]{:S(2)}) async-start(), calls=%async_computation | async-start | bytes 131072 | tf_op jit(solution)/shard_map/psum | solution.py:76
  136.5 10.6 %copy-start.3 = (s32[256]{0:T(256)S(1)}, s32[256]{0:T(256)}, u32[]{:S(2)}) copy-start(s32[256]{0:T(256)} %param.22) | copy-start | bytes 3076
  136.5 15.9 %copy-start.2 = (bf16[256,128]{1,0:T(8,128)(2,1)S(1)}, bf16[256,128]{1,0:T(8,128)(2,1)}, u32[]{:S(2)}) copy-start(bf16[256,128]{1,0:T(8,128)(2,1)} %param.15) | copy-start | bytes 196612
  136.5 18.0 %copy-start.4 = (bf16[256,128]{1,0:T(8,128)(2,1)S(1)}, bf16[256,128]{1,0:T(8,128)(2,1)}, u32[]{:S(2)}) copy-start(bf16[256,128]{1,0:T(8,128)(2,1)} %param.16) | copy-start | bytes 196612
  136.5 21.3 %copy-start.5 = (s32[8]{0:T(128)S(1)}, s32[8]{0:T(128)}, u32[]{:S(2)}) copy-start(s32[8]{0:T(128)} %param.23) | copy-start | bytes 100
  136.5 70.5 %copy-start.1 = (bf16[256,1024]{1,0:T(8,128)(2,1)S(1)}, bf16[256,1024]{1,0:T(8,128)(2,1)}, u32[]{:S(2)}) copy-start(bf16[256,1024]{1,0:T(8,128)(2,1)} %param.14) | copy-start | bytes 1572868
  145.8 111.5 %all-gather.5.cloned.1.call-start = ((), (), s32[]{:S(2)}) async-start(), calls=%async_computation.1 | async-start | bytes 4456448 | tf_op jit(solution)/shard_map/all_gather | solution.py:114
  146.6 164.1 %all-gather.7.cloned.1.call-start = ((), (), s32[]{:S(2)}) async-start(), calls=%async_computation.2 | async-start | bytes 4456448 | tf_op jit(solution)/shard_map/all_gather | solution.py:115
  147.8 31.4 %collective-permute-start = (bf16[256]{0:T(256)(128)(2,1)S(1)}, bf16[256]{0:T(256)(128)(2,1)S(1)}, u32[]{:S(2)}, u32[]{:S(2)}) collective-permute-start(bf16[256]{0:T(256)(128)(2,1)S(1)} %get-tuple-element.107), channel_id=1, source_target_pairs={{0,8},{8,16},{16,24},{24,32},{32,40},{40,48},{48,56},{56,64},{64,7... | collective-permute-start | bytes 1544 | tf_op jit(solution)/shard_map/ppermute | solution.py:18
  152.4 55.0 %collective-permute-start.1 = (bf16[256,128]{1,0:T(8,128)(2,1)S(1)}, bf16[256,128]{1,0:T(8,128)(2,1)S(1)}, u32[]{:S(2)}, u32[]{:S(2)}) collective-permute-start(bf16[256,128]{1,0:T(8,128)(2,1)S(1)} %copy-done.2), channel_id=1, source_target_pairs={{0,8},{8,16},{16,24},{24,32},{32,40},{40,48},{48,56},{56,64},{64,7... | collective-permute-start | bytes 196616 | tf_op jit(solution)/shard_map/ppermute | solution.py:18
  154.7 54.6 %collective-permute-start.2 = (bf16[256,128]{0,1:T(8,128)(2,1)S(1)}, bf16[256,128]{0,1:T(8,128)(2,1)S(1)}, u32[]{:S(2)}, u32[]{:S(2)}) collective-permute-start(bf16[256,128]{0,1:T(8,128)(2,1)S(1)} %copy.32), channel_id=1, source_target_pairs={{0,8},{8,16},{16,24},{24,32},{32,40},{40,48},{48,56},{56,64},{64,7... | collective-permute-start | bytes 196616 | tf_op jit(solution)/shard_map/ppermute | solution.py:18
Sparse Core Ops, SparseCore 0:
  9.7 111.7 all-gather.8
  146.0 60.2 all-reduce.1
  208.6 48.6 all-gather.4
  259.5 51.0 all-gather.6
where the time goes:
time: 440 us; the launch traced here: 436 us
  waiting for transfers between devices  236 us (54%)
  matrix products  96.2 us (22%)
  other arithmetic  34.6 us (8%)
  local copies, waits for them, and re-layouts  23.4 us (5%)
  blocking collectives  21.3 us (5%)
  between operations  13.4 us (3%)
  starting transfers between devices  9.94 us (2%)
    all_gather x1, waiting for transfers between devices, per_device(): piece = lax.all_gather(flat_store, 'ctx', axis=0, tiled=True)  107 us
    all_gather x1, waiting for transfers between devices, per_device(): value_matrix = lax.all_gather(cached_value_rows, 'ctx', axis=0, tiled=True)  53.4 us
    dot_general x17, matrix products, update_softmax(): jnp.einsum('tkgn,nkd->tkgd', weights.astype(jnp.bfloat16), value_three, p...  48.5 us
    all_gather x1, waiting for transfers between devices, per_device(): key_matrix = lax.all_gather(cached_key_rows, 'ctx', axis=0, tiled=True)  47 us
    dot_general x17, matrix products, update_softmax(): jnp.einsum('tkgd,nkd->tkgn', query_rows, key_three, preferred_element_typ...  38.3 us
    reduce_sum x17, other arithmetic, update_softmax(): run_sum = run_sum * fading + jnp.sum(weights, axis=-1)  28.2 us
    psum x1, waiting for transfers between devices, per_device(): lax.psum(rank_acts.reshape(tok_rows, 2 * rank_size).astype(jnp.bfloat16),...  26.8 us
    all_gather x1, blocking collectives, per_device(): doc_piece = lax.all_gather(doc_rows, 'ctx', axis=0, tiled=True)  21.3 us
  transfers between devices with their start and end apart: 7, of which 4 were waited for; matrix products, arithmetic and copies ran while one was open for 2% of the time, Pallas kernels for 0%

commit v1 on v0

v1 whole, which is shorter than its diff:
```python
import functools
import math

import jax
import jax.numpy as jnp
from jax import lax
from jax.experimental import pallas as pl
from jax.experimental.pallas import tpu as pltpu
from jax.sharding import PartitionSpec as P

HEAD_SIZE = 128
PAGE = 128
SIDE = 4
HALF_ROWS = 1040
TILE = 32
GROUP = 4
VMEM_LIMIT = 56 * 1024 * 1024

adapter_scale = 2.0


def pull(block, dx, dy):
    route = []
    for i in range(SIDE * SIDE):
        y, x = divmod(i, SIDE)
        route.append((((y + dy) % SIDE) * SIDE + (x + dx) % SIDE, i))
    return lax.ppermute(block, "ctx", route)


def pull_tp(block, dz, dc):
    route = []
    for i in range(2 * SIDE):
        z, c = divmod(i, 2)
        route.append((((z + dz) % SIDE) * 2 + (c ^ dc), i))
    return lax.ppermute(block, "tp", route)


def pick_kernel(index_ref, b0, b1, b2, b3, o0, o1, o2, o3, sems):
    bufs, outs = (b0, b1, b2, b3), (o0, o1, o2, o3)
    for k in range(8):
        index = index_ref[k]
        row = lax.rem(index, 4)
        for b in range(4):
            @pl.when(index // 4 == b)
            def _():
                pltpu.make_async_copy(bufs[b].at[row], outs[k // 2].at[k % 2], sems.at[k]).start()
    for k in range(8):
        pltpu.make_async_copy(bufs[0].at[0], outs[k // 2].at[k % 2], sems.at[k]).wait()


def pick(index, bufs):
    rank, width = bufs[0].shape[1:]
    out = jax.ShapeDtypeStruct((2, rank, width), jnp.bfloat16)
    return pl.pallas_call(
        pick_kernel,
        out_shape=[out] * 4,
        in_specs=[pl.BlockSpec(memory_space=pltpu.SMEM)] + [pl.BlockSpec(memory_space=pl.ANY)] * 4,
        out_specs=[pl.BlockSpec(memory_space=pl.ANY)] * 4,
        scratch_shapes=[pltpu.SemaphoreType.DMA((8,))],
        name="pick_items",
    )(index, *bufs)


def route_adapter(raw, rows_of, me_along, me_across, along_x):
    def first(v, d):
        return pull(v, d, 0) if along_x else pull(v, 0, d)

    def second(v, d):
        return pull(v, 0, d) if along_x else pull(v, d, 0)

    ring = [raw, first(raw, 1), first(raw, 2), first(raw, -1)]
    index = []
    for d in range(4):
        there = (me_across + d) % SIDE
        dest = there * SIDE + me_along if along_x else me_along * SIDE + there
        for k in range(2):
            row = rows_of[dest + k]
            owner = row // 4
            owner_along = owner % SIDE if along_x else owner // SIDE
            index.append(((owner_along - me_along + SIDE) % SIDE) * 4 + row % 4)
    items = pick(jnp.stack(index).astype(jnp.int32), ring)
    got = [items[0], second(items[3], 1), second(items[2], 2), second(items[1], -1)]
    me = me_across * SIDE + me_along if along_x else me_along * SIDE + me_across
    blocks = []
    for k in range(2):
        owner = rows_of[me + k] // 4
        owner_across = owner // SIDE if along_x else owner % SIDE
        source = (owner_across - me_across + SIDE) % SIDE
        block = got[0][k]
        for d in range(1, 4):
            block = jnp.where(source == d, got[d][k], block)
        blocks.append(block)
    return jnp.concatenate(blocks, axis=0)


def spread(own):
    east, west = pull(own, 1, 0), pull(own, -1, 0)
    south, north = pull(own, 0, 1), pull(own, 0, -1)
    lo = lambda v: v[0:1]
    hi = lambda v: v[1:2]
    join = lambda *v: jnp.concatenate(v, axis=0)
    e2 = pull(join(lo(east), lo(south), hi(north)), 1, 0)
    w2 = pull(join(hi(west), hi(south), lo(north)), -1, 0)
    s2 = pull(join(lo(south), hi(east), lo(west)), 0, 1)
    n2 = pull(join(hi(north), lo(east), hi(west)), 0, -1)
    e3, w3 = pull(e2[1:], 1, 0), pull(w2[1:], -1, 0)
    s3, n3 = pull(s2[1:], 0, 1), pull(n2[1:], 0, -1)
    e4 = pull(n3[0:1], 1, 0)
    s4 = pull(w3[0:1], 0, 1)
    return (own, east, west, south, north), (e2, w2, s2, n2), (e3, w3, s3, n3), (e4, s4)


def owners(bufs):
    return jnp.concatenate([b[:, 1024, :4].reshape(-1) for b in bufs]).astype(jnp.int32)


LOG_SCALE = math.log2(math.e) / math.sqrt(HEAD_SIZE)


def soft_step(q, keys, values, m_ref, al_ref, rows, mask=None):
    scores = lax.dot_general(q, keys, (((1,), (1,)), ((), ())), preferred_element_type=jnp.float32)
    scores = scores * LOG_SCALE
    if mask is not None:
        scores = jnp.where(mask, scores, -1e30)
    count = scores.shape[1] // 128
    parts = [scores[:, i * 128:(i + 1) * 128] for i in range(count)]
    peak = functools.reduce(jnp.maximum, parts)
    peak = jnp.max(peak, axis=1, keepdims=True)
    old = m_ref[rows, :]
    new = jnp.maximum(old, peak)
    fade = jnp.exp2(old - new)
    weights = jnp.concatenate([jnp.exp2(s - new).astype(jnp.bfloat16) for s in parts], axis=1)
    added = jnp.dot(weights, values, preferred_element_type=jnp.float32)
    m_ref[rows, :] = new
    al_ref[rows, 0:128] = al_ref[rows, 0:128] * fade + added[:, 0:128]
    al_ref[rows, 128:256] = al_ref[rows, 128:256] * fade + added[:, 128:256]


def attend_kernel(first, last, sizes, *refs):
    info_ref, q_ref = refs[0], refs[1]
    pos = 2
    if first:
        span_ref, prev_ref = refs[pos:pos + 2]
        pos += 2
    else:
        m_in, al_in = refs[pos:pos + 2]
        pos += 2
    bufs = refs[pos:pos + len(sizes)]
    pos += len(sizes)
    if last:
        out_ref = refs[pos]
        pos += 1
    else:
        m_out, al_out = refs[pos:pos + 2]
        pos += 2
    k_sc, v_sc, count_sc, m_sc, al_sc, m_keep, al_keep = refs[pos:]
    rows_tile = TILE * 8
    tiles = q_ref.shape[0] // rows_tile
    seg_a, cut, prev_cut = info_ref[0], info_ref[1], info_ref[2]

    if first:
        m_sc[...] = jnp.full(m_sc.shape, -1e30, jnp.float32)
        al_sc[...] = jnp.zeros(al_sc.shape, jnp.float32)
        v_sc[0, :, 128:256] = jnp.ones((v_sc.shape[1], 128), jnp.bfloat16)
        v_sc[0, 0:256, 0:128] = prev_ref[256:512, :]
        v_sc[0, 256:512, 0:128] = span_ref[256:512, :]
        k_sc[0, 0:256, :] = prev_ref[0:256, :]
        k_sc[0, 256:512, :] = span_ref[0:256, :]

        @pl.loop(0, tiles)
        def _(t):
            rows = pl.ds(pl.multiple_of(t * rows_tile, rows_tile), rows_tile)
            token = t * TILE + lax.broadcasted_iota(jnp.int32, (rows_tile, 512), 0) % TILE
            key = lax.broadcasted_iota(jnp.int32, (rows_tile, 512), 1) - 256
            in_a = token < cut
            mask = ((key < 0) & in_a & (key + 256 >= prev_cut)) | (
                (key >= 0) & (key <= token) & ((key < cut) == in_a)
            )
            soft_step(q_ref[rows, :], k_sc[0, 0:512, :], v_sc[0, 0:512, :], m_sc, al_sc, rows, mask)
    else:
        m_sc[...] = m_in[...]
        al_sc[...] = al_in[...]

    v_sc[0, :, 128:256] = jnp.ones((v_sc.shape[1], 128), jnp.bfloat16)
    v_sc[1, :, 128:256] = jnp.ones((v_sc.shape[1], 128), jnp.bfloat16)
    count_sc[0] = 0
    count_sc[1] = 0
    base = 3
    for buf, halves in zip(bufs, sizes):
        @pl.loop(0, halves * 4)
        def _(i, buf=buf, base=base):
            which = info_ref[base + i] - seg_a

            @pl.when((which == 0) | (which == 1))
            def _():
                n = count_sc[which]
                there = pl.ds(pl.multiple_of(n * PAGE, PAGE), PAGE)
                h, page = i // 4, i % 4
                k_sc[which, there, :] = buf[h, pl.ds(pl.multiple_of(page * PAGE, PAGE), PAGE), :]
                v_sc[which, there, 0:128] = buf[
                    h, pl.ds(pl.multiple_of(512 + page * PAGE, PAGE), PAGE), :
                ]
                count_sc[which] = n + 1
        base += halves * 4

    for side in range(2):
        n = count_sc[side]
        full = ((n + GROUP - 1) // GROUP) * GROUP

        @pl.loop(n, full)
        def _(i, side=side):
            there = pl.ds(pl.multiple_of(i * PAGE, PAGE), PAGE)
            k_sc[side, there, :] = k_sc[side, 0:PAGE, :]
            v_sc[side, there, :] = jnp.zeros((PAGE, 256), jnp.bfloat16)

        low = 0 if side == 0 else cut // TILE
        high = (cut + TILE - 1) // TILE if side == 0 else tiles
        high = jnp.where(n > 0, high, low)

        @pl.loop(low, high)
        def _(t, side=side, full=full):
            rows = pl.ds(pl.multiple_of(t * rows_tile, rows_tile), rows_tile)
            mixed = (t * TILE < cut) & ((t + 1) * TILE > cut)

            @pl.when(mixed)
            def _():
                m_keep[...] = m_sc[rows, :]
                al_keep[...] = al_sc[rows, :]

            @pl.loop(0, full // GROUP)
            def _(g):
                there = pl.ds(pl.multiple_of(g * (GROUP * PAGE), GROUP * PAGE), GROUP * PAGE)
                soft_step(q_ref[rows, :], k_sc[side, there, :], v_sc[side, there, :], m_sc, al_sc, rows)

            @pl.when(mixed)
            def _():
                token = t * TILE + lax.broadcasted_iota(jnp.int32, (rows_tile, 128), 0) % TILE
                mine = (token < cut) if side == 0 else (token >= cut)
                m_sc[rows, :] = jnp.where(mine, m_sc[rows, :], m_keep[...])
                for c in range(2):
                    cols = slice(c * 128, (c + 1) * 128)
                    al_sc[rows, cols] = jnp.where(mine, al_sc[rows, cols], al_keep[:, cols])

    if last:
        for t in range(tiles):
            for h in range(8):
                rows = slice((t * 8 + h) * TILE, (t * 8 + h + 1) * TILE)
                out = al_sc[rows, 0:128] / al_sc[rows, 128:256]
                out_ref[t * TILE:(t + 1) * TILE, h * 128:(h + 1) * 128] = out.astype(jnp.bfloat16)
    else:
        m_out[...] = m_sc[...]
        al_out[...] = al_sc[...]


def attend(info, q, span, state, bufs, last):
    first = state is None
    sizes = tuple(b.shape[0] for b in bufs)
    pages = 4 * sum(sizes)
    pages = max(((pages + GROUP - 1) // GROUP) * GROUP, 4)
    rows = q.shape[0]
    state_shape = [
        jax.ShapeDtypeStruct((rows, 128), jnp.float32),
        jax.ShapeDtypeStruct((rows, 256), jnp.float32),
    ]
    vmem = pl.BlockSpec(memory_space=pltpu.VMEM)
    args = [info, q] + (list(span) if first else list(state)) + list(bufs)
    out_shape = jax.ShapeDtypeStruct((rows // 8, 1024), jnp.bfloat16) if last else state_shape
    return pl.pallas_call(
        functools.partial(attend_kernel, first, last, sizes),
        out_shape=out_shape,
        in_specs=[pl.BlockSpec(memory_space=pltpu.SMEM)] + [vmem] * (len(args) - 1),
        out_specs=vmem if last else [vmem, vmem],
        scratch_shapes=[
            pltpu.VMEM((2, pages * PAGE, 128), jnp.bfloat16),
            pltpu.VMEM((2, pages * PAGE, 256), jnp.bfloat16),
            pltpu.SMEM((2,), jnp.int32),
            pltpu.VMEM((rows, 128), jnp.float32),
            pltpu.VMEM((rows, 256), jnp.float32),
            pltpu.VMEM((TILE * 8, 128), jnp.float32),
            pltpu.VMEM((TILE * 8, 256), jnp.float32),
        ],
        compiler_params=pltpu.CompilerParams(vmem_limit_bytes=VMEM_LIMIT),
        name="attend_last" if last else ("attend_first" if first else "attend_mid"),
    )(*args)


def per_device(
    tokens_in,
    base_queries,
    fresh_keys,
    fresh_values,
    cached_key_rows,
    cached_value_rows,
    adapter_store,
    adapter_slot,
    segment_adapter,
    token_request,
    cache_doc,
):
    tok_rows = tokens_in.shape[0]
    me = lax.axis_index("ctx")
    me_y, me_x = me // SIDE, me % SIDE
    rows_of = adapter_slot[segment_adapter]
    seg_a = token_request[0]
    cut = jnp.sum((token_request == seg_a).astype(jnp.int32))

    down = route_adapter(adapter_store[:, 0], rows_of, me_x, me_y, True)
    up = route_adapter(adapter_store[:, 1], rows_of, me_y, me_x, False)

    def half(k):
        ids = jnp.pad(cache_doc[k * 4:k * 4 + 4], (0, 124)).astype(jnp.bfloat16)
        return jnp.concatenate(
            [
                cached_key_rows[k * 512:(k + 1) * 512],
                cached_value_rows[k * 512:(k + 1) * 512],
                jnp.broadcast_to(ids[None], (16, 128)),
            ],
            axis=0,
        )

    own = jnp.stack([half(0), half(1)])
    stages = spread(own)
    span = jnp.concatenate(
        [fresh_keys, fresh_values, jnp.broadcast_to(cut.astype(jnp.bfloat16), (16, 128))], axis=0
    )
    prev = lax.ppermute(span, "ctx", [(i - 1, i) for i in range(1, SIDE * SIDE)])
    prev_cut = jnp.where(me == 0, tok_rows, prev[512, 0].astype(jnp.int32))

    in_a = (jnp.arange(tok_rows) < cut)[:, None]
    acts = jnp.dot(tokens_in, down.T, preferred_element_type=jnp.float32)
    acts = jnp.where(in_a, acts[:, :64], acts[:, 64:]).astype(jnp.bfloat16)
    acts = jnp.concatenate([acts[:tok_rows // 2], acts[tok_rows // 2:]], axis=1)
    acts = (acts.astype(jnp.float32) + pull_tp(acts, 0, 1).astype(jnp.float32)).astype(jnp.bfloat16)
    total = acts.astype(jnp.float32)
    for dz in (1, 2, 3):
        total = total + pull_tp(acts, dz, 0).astype(jnp.float32)
    total = jnp.concatenate([total[:, :64], total[:, 64:]], axis=0).astype(jnp.bfloat16)
    zero = jnp.zeros_like(total)
    total = jnp.concatenate([jnp.where(in_a, total, zero), jnp.where(in_a, zero, total)], axis=1)
    lora = jnp.dot(total, up, preferred_element_type=jnp.float32)
    query = (base_queries.astype(jnp.float32) + adapter_scale * lora).astype(jnp.bfloat16)
    query = query.reshape(tok_rows // TILE, TILE, 8, HEAD_SIZE).transpose(0, 2, 1, 3)
    query = query.reshape(tok_rows * 8, HEAD_SIZE)

    def info(bufs):
        return jnp.concatenate([jnp.stack([seg_a, cut, prev_cut]), owners(bufs)])

    state = attend(info(stages[0]), query, (span, prev), None, stages[0], False)
    state = attend(info(stages[1]), query, None, state, stages[1], False)
    late = stages[2] + stages[3]
    return attend(info(late), query, None, state, late, True)


def solution(mesh):
    in_specs = (
        P("ctx", "tp"),
        P("ctx", "tp"),
        P("ctx", "tp"),
        P("ctx", "tp"),
        P("ctx", "tp"),
        P("ctx", "tp"),
        P("ctx", None, None, "tp"),
        P(),
        P(),
        P("ctx"),
        P("ctx"),
    )
    out_specs = P("ctx", "tp")
    return jax.shard_map(
        per_device, mesh=mesh, in_specs=in_specs, out_specs=out_specs, check_vma=False
    )
```

time: 440 us -> 306 us (0.70)
  waiting for transfers between devices: 236 us -> 36.7 us
  Pallas kernels: 0 us -> 147 us
  matrix products: 96.2 us -> 0.63 us
  between operations: 13.4 us -> 47.4 us
  starting transfers between devices: 9.94 us -> 40.5 us
  other arithmetic: 34.6 us -> 9.41 us
  blocking collectives: 21.3 us -> 0 us
  local copies, waits for them, and re-layouts: 23.4 us -> 18.6 us
    all_gather x3 -> x0, waiting for transfers between devices: 208 us -> none  [the longest x1 107 us: per_device(): piece = lax.all_gather(flat_store, 'ctx', axis=0, tiled=True)]
    pallas_call x0 -> x5, Pallas kernels: none -> 147 us  [the longest x3 80.1 us: attend(): pl.pallas_call(functools.partial(attend_kernel, first, last, sizes), out_...]
    dot_general x37 -> x2, matrix products: 96.2 us -> 0.63 us  [the longest x1 0.32 us: per_device(): lora = jnp.dot(total, up, preferred_element_type=jnp.float32)]
    ppermute x3 -> x31, waiting for transfers between devices: 0.01 us -> 36.7 us  [the longest x1 18.5 us: per_device(): lax.ppermute(span, 'ctx', [(i - 1, i) for i in range(1, SIDE * SIDE)])]
    ppermute x3 -> x31, starting transfers between devices: 9.82 us -> 40.5 us  [the longest x26 31.3 us: pull(): return lax.ppermute(block, 'ctx', route)]
    reduce_sum x17 -> x1, other arithmetic: 28.2 us -> 1.29 us  [per_device(): cut = jnp.sum((token_request == seg_a).astype(jnp.int32))]
    psum x1 -> x0, waiting for transfers between devices: 26.8 us -> none  [per_device(): lax.psum(rank_acts.reshape(tok_rows, 2 * rank_size).astype(jnp.bfloat16),...]
    all_gather x1 -> x0, blocking collectives: 21.3 us -> none  [per_device(): doc_piece = lax.all_gather(doc_rows, 'ctx', axis=0, tiled=True)]
  transfers between devices with their start and end apart: 7 -> 31, of which waited for: 4 -> 6; matrix products, arithmetic and copies ran while one was open for 2% -> 8% of each run, Pallas kernels for 0% -> 41%
where the time goes in v1:
time: 306 us; the launch traced here: 301 us
  Pallas kernels  147 us (48%)
  between operations  47.4 us (15%)
  starting transfers between devices  40.5 us (13%)
  waiting for transfers between devices  36.7 us (12%)
  local copies, waits for them, and re-layouts  18.6 us (6%)
  other arithmetic  9.41 us (3%)
    pallas_call x3, Pallas kernels, attend(): pl.pallas_call(functools.partial(attend_kernel, first, last, sizes), out_...  80.1 us
    pallas_call x2, Pallas kernels, pick(): pl.pallas_call(pick_kernel, out_shape=[out] * 4, in_specs=[pl.BlockSpec(m...  67.2 us
    ppermute x26, starting transfers between devices, pull(): return lax.ppermute(block, 'ctx', route)  31.3 us
    ppermute x1, waiting for transfers between devices, per_device(): lax.ppermute(span, 'ctx', [(i - 1, i) for i in range(1, SIDE * SIDE)])  18.5 us
    ppermute x26, waiting for transfers between devices, pull(): return lax.ppermute(block, 'ctx', route)  14.8 us
  transfers between devices with their start and end apart: 31, of which 6 were waited for; matrix products, arithmetic and copies ran while one was open for 8% of the time, Pallas kernels for 41%

profile of v1, /device:TPU:22, one launch (start us, length us, event | category | flops | bytes accessed | tf_op | source)
XLA Modules:
  0.0 300.7 jit_solution(15418194150466124635)
XLA Ops:
  0.1 2.2 slice_bitcast_fusion.1
  2.2 0.8 collective-permute-start.15
  3.1 1.1 collective-permute-start.16
  4.2 2.1 collective-permute-start.17
  6.3 0.4 collective-permute-start.25
  6.7 0.6 slice.191
  7.3 1.3 fusion.26
  9.2 0.1 maximum_maximum_fusion.refs_2_
  9.4 3.8 %collective-permute-start = (bf16[528,128]{1,0:T(8,128)(2,1)S(1)}, bf16[528,128]{1,0:T(8,128)(2,1)S(1)}, u32[]{:S(2)}, u32[]{:S(2)}) collective-permute-start(bf16[528,128]{1,0:T(8,128)(2,1)S(1)} %maximum_maximum_fusion.refs_2_), channel_id=1, source_target_pairs={{0,8},{8,16},{16,24},{24,32},{32,40},{40,48},{48,56},{56,64},{64,7... | collective-permute-start | bytes 405512 | tf_op jit(solution)/shard_map/ppermute | solution.py:326
  13.4 18.5 %collective-permute-done.refs_3_ = bf16[528,128]{1,0:T(8,128)(2,1)S(1)} collective-permute-done((bf16[528,128]{1,0:T(8,128)(2,1)S(1)}, bf16[528,128]{1,0:T(8,128)(2,1)S(1)}, u32[]{:S(2)}, u32[]{:S(2)}) %collective-permute-start) | collective-permute-done | bytes 135200 | tf_op jit(solution)/shard_map/ppermute | solution.py:326
  31.9 0.3 collective-permute-start.26
  32.3 0.8 collective-permute-start.1
  33.2 2.2 collective-permute-start.27
  35.4 2.5 collective-permute-start.6
  37.9 0.9 collective-permute-start.2
  38.9 9.7 %collective-permute-done.26.b2 = bf16[4,64,1024]{2,1,0:T(8,128)(2,1)} collective-permute-done((bf16[4,64,1024]{2,1,0:T(8,128)(2,1)}, bf16[4,64,1024]{2,1,0:T(8,128)(2,1)}, u32[]{:S(2)}, u32[]{:S(2)}) %collective-permute-start.26) | collective-permute-done | bytes 524320 | tf_op jit(solution)/shard_map/ppermute | solution.py:27
  48.6 1.3 collective-permute-start.3
  49.9 0.7 gather_fusion
  50.6 0.8 fusion.38
  97.1 0.7 stack.86.index_ref
  97.7 0.6 stack.95.index_ref
  98.3 0.6 iota_compare_fusion
  98.9 0.6 slice.254
  100.2 33.6 %pick_items.2 = (bf16[2,64,1024]{2,1,0:T(8,128)(2,1)}, bf16[2,64,1024]{2,1,0:T(8,128)(2,1)}, bf16[2,64,1024]{2,1,0:T(8,128)(2,1)}, bf16[2,64,1024]{2,1,0:T(8,128)(2,1)}) custom-call(s32[8]{0:T(128)} %stack.86.index_ref, bf16[4,64,1024]{2,1,0:T(8,128)(2,1)} %copy-done.9, bf16[4,64,1024]{2,1,0:T(8,128)(2,1)} %collective-permute-done.15.b1, ...), custom_call_target="tpu_custom_call" | custom-call | tf_op jit(solution)/shard_map/pick_items/pallas_call | solution.py:54
  133.9 0.3 collective-permute-start.18
  134.2 33.6 %pick_items.3 = (bf16[2,64,1024]{2,1,0:T(8,128)(2,1)}, bf16[2,64,1024]{2,1,0:T(8,128)(2,1)}, bf16[2,64,1024]{2,1,0:T(8,128)(2,1)}, bf16[2,64,1024]{2,1,0:T(8,128)(2,1)}) custom-call(s32[8]{0:T(128)} %stack.95.index_ref, bf16[4,64,1024]{2,1,0:T(8,128)(2,1)} %get-tuple-element.34.b0, bf16[4,64,1024]{2,1,0:T(8,128)(2,1)} %collective-permute-done.25.b1, ...), custom_call_target="tpu_custom_call" | custom-call | tf_op jit(solution)/shard_map/pick_items/pallas_call | solution.py:54
  167.8 2.0 collective-permute-start.19
  170.0 1.1 collective-permute-start.20
  171.2 2.5 collective-permute-start.28
  173.7 0.3 collective-permute-start.29
  174.0 0.7 slice_reduce_fusion.4
  175.0 1.1 fusion.33
  176.2 1.5 pad_maximum_fusion.3
  177.7 0.6 collective-permute-start.30
  178.4 2.6 collective-permute-start.4
  181.0 1.3 fusion.20
  182.3 0.3 convolution_bitcast_fusion
  182.8 1.8 pad_add_fusion.3
  184.6 3.3 %collective-permute-start.7 = (bf16[3,1040,128]{2,1,0:T(8,128)(2,1)}, bf16[3,1040,128]{2,1,0:T(8,128)(2,1)S(1)}, u32[]{:S(2)}, u32[]{:S(2)}) collective-permute-start(bf16[3,1040,128]{2,1,0:T(8,128)(2,1)} %get-tuple-element.48), channel_id=1, source_target_pairs={{24,0},{0,8},{8,16},{16,24},{56,32},{32,40},{40,48},{48,56},{88,64... | collective-permute-start | bytes 2396168 | tf_op jit(solution)/shard_map/ppermute | solution.py:27
  187.9 4.1 %collective-permute-start.22 = (bf16[128,128]{0,1:T(8,128)(2,1)S(1)}, bf16[128,128]{0,1:T(8,128)(2,1)S(1)}, u32[]{:S(2)}, u32[]{:S(2)}) collective-permute-start(bf16[128,128]{0,1:T(8,128)(2,1)S(1)} %add_convert_fusion.1), channel_id=1, source_target_pairs={{2,0},{3,1},{4,2},{5,3},{6,4},{7,5},{0,6},{1,7},{10,8},{11,9},{12,... | collective-permute-start | bytes 98312 | tf_op jit(solution)/shard_map/ppermute | solution.py:35
  192.1 1.3 collective-permute-start.24
  193.4 0.3 collective-permute-done.22
  193.7 0.7 collective-permute-start.9
  194.4 3.2 %collective-permute-done.23 = bf16[128,128]{0,1:T(8,128)(2,1)S(1)} collective-permute-done((bf16[128,128]{0,1:T(8,128)(2,1)S(1)}, bf16[128,128]{0,1:T(8,128)(2,1)S(1)}, u32[]{:S(2)}, u32[]{:S(2)}) %collective-permute-start.23) | collective-permute-done | bytes 32800 | tf_op jit(solution)/shard_map/ppermute | solution.py:35
  197.5 0.9 collective-permute-start.11
  198.5 0.3 fusion.2
  198.9 0.9 copy.17
  199.8 27.8 %attend_first.1 = (f32[2048,128]{1,0:T(8,128)}, f32[2048,256]{1,0:T(8,128)}) custom-call(s32[43]{0:T(128)} %get-tuple-element.29.refs_0_, bf16[2048,128]{1,0:T(8,128)(2,1)} %bitcast.73, bf16[528,128]{1,0:T(8,128)(2,1)} %copy-done.11, bf16[528,128]{1,0:T(8,128)(2,1)} %copy-done.21, bf16[2,1040,128]{2,1,0:T(8,128)(2,1)} %copy-done.5, ...), custom_call_target="tpu_custom_call" | custom-call | tf_op jit(solution)/shard_map/attend_first/pallas_call | solution.py:268
  227.8 1.0 slice.263
  228.7 1.9 slice.269
  230.8 1.0 slice.258
  231.8 2.0 collective-permute-start.5
  233.8 0.7 slice_reduce_fusion
  234.7 2.1 collective-permute-start.10
  236.9 1.8 pad_add_fusion.2.refs_0_
  238.7 28.2 %attend_mid.1 = (f32[2048,128]{1,0:T(8,128)}, f32[2048,256]{1,0:T(8,128)}) custom-call(s32[51]{0:T(128)} %pad_add_fusion.2.refs_0_, bf16[2048,128]{1,0:T(8,128)(2,1)} %bitcast.74, f32[2048,128]{1,0:T(8,128)} %get-tuple-element.25.refs_2_, f32[2048,256]{1,0:T(8,128)} %get-tuple-element.26.refs_3_, bf16[3,1040,128]{2,1,0:T(8,128)(2,1)} %copy-done.2, ...), custom_call_target="tpu_custom_call" | custom-call | tf_op jit(solution)/shard_map/attend_mid/pallas_call | solution.py:268
  267.0 1.1 slice.271
  268.1 0.7 slice_reduce_fusion.8
  268.8 0.7 slice_reduce_fusion.11
  269.5 0.8 copy-done.12
  270.7 2.7 collective-permute-done.14.refs_9_
  273.4 2.4 collective-permute-done.13.refs_8_
  275.8 0.6 pad_add_fusion.refs_0_
  276.4 24.2 %attend_last.1 = bf16[256,1024]{1,0:T(8,128)(2,1)} custom-call(s32[43]{0:T(128)} %pad_add_fusion.refs_0_, bf16[2048,128]{1,0:T(8,128)(2,1)} %bitcast.75, f32[2048,128]{1,0:T(8,128)} %get-tuple-element.27.refs_2_, f32[2048,256]{1,0:T(8,128)} %get-tuple-element.28.refs_3_, bf16[2,1040,128]{2,1,0:T(8,128)(2,1)} %collective-permute-done.5.refs_4_, ...), custom_call_target="tpu_custom_call" | custom-call | tf_op jit(solution)/shard_map/attend_last/pallas_call | solution.py:268
  (143 shorter events, 2.7 us)
Async XLA Ops:
  0.0 182.3 %copy-start = (bf16[256,1024]{1,0:T(8,128)(2,1)S(1)}, bf16[256,1024]{1,0:T(8,128)(2,1)}, u32[]{:S(2)}) copy-start(bf16[256,1024]{1,0:T(8,128)(2,1)} %param.11) | copy-start | bytes 1572868
  0.0 6.7 %copy-start.24 = (s32[256]{0:T(256)S(1)}, s32[256]{0:T(256)}, u32[]{:S(2)}) copy-start(s32[256]{0:T(256)} %param.20) | copy-start | bytes 3076
  0.0 9.2 %copy-start.23 = (bf16[256,128]{1,0:T(8,128)(2,1)S(1)}, bf16[256,128]{1,0:T(8,128)(2,1)}, u32[]{:S(2)}) copy-start(bf16[256,128]{1,0:T(8,128)(2,1)} %param.13) | copy-start | bytes 196612
  0.0 9.2 %copy-start.22 = (bf16[256,128]{1,0:T(8,128)(2,1)S(1)}, bf16[256,128]{1,0:T(8,128)(2,1)}, u32[]{:S(2)}) copy-start(bf16[256,128]{1,0:T(8,128)(2,1)} %param.14) | copy-start | bytes 196612
  0.0 13.2 %copy-start.17 = (bf16[1024,128]{1,0:T(8,128)(2,1)S(1)}, bf16[1024,128]{1,0:T(8,128)(2,1)}, u32[]{:S(2)}) copy-start(bf16[1024,128]{1,0:T(8,128)(2,1)} %param.15) | copy-start | bytes 786436
  0.0 13.2 %copy-start.18 = (bf16[1024,128]{1,0:T(8,128)(2,1)S(1)}, bf16[1024,128]{1,0:T(8,128)(2,1)}, u32[]{:S(2)}) copy-start(bf16[1024,128]{1,0:T(8,128)(2,1)} %param.16) | copy-start | bytes 786436
  0.0 13.2 %copy-start.26 = (s32[8]{0:T(128)S(1)}, s32[8]{0:T(128)}, u32[]{:S(2)}) copy-start(s32[8]{0:T(128)} %param.21) | copy-start | bytes 100
  2.2 33.1 %copy-start.9 = (bf16[4,64,1024]{2,1,0:T(8,128)(2,1)}, bf16[4,64,1024]{2,1,0:T(8,128)(2,1)S(1)}, u32[]{:S(2)}) copy-start(bf16[4,64,1024]{2,1,0:T(8,128)(2,1)S(1)} %get-tuple-element.33.b0) | copy-start | bytes 1572868
  2.2 36.6 %copy-start.27 = (s32[17]{0:T(128)S(1)}, s32[17]{0:T(128)}, u32[]{:S(2)}) copy-start(s32[17]{0:T(128)} %param.19) | copy-start | bytes 208
  2.2 47.6 %copy-start.1 = (s32[64]{0:T(128)S(1)}, s32[64]{0:T(128)}, u32[]{:S(2)}) copy-start(s32[64]{0:T(128)} %param.18) | copy-start | bytes 772
  2.2 30.1 %collective-permute-start.15 = (bf16[4,64,1024]{2,1,0:T(8,128)(2,1)S(1)}, bf16[4,64,1024]{2,1,0:T(8,128)(2,1)}, u32[]{:S(2)}, u32[]{:S(2)}) collective-permute-start(bf16[4,64,1024]{2,1,0:T(8,128)(2,1)S(1)} %get-tuple-element.33.b0), channel_id=1, source_target_pairs={{8,0},{16,8},{24,16},{0,24},{40,32},{48,40},{56,48},{32,56},{72,64... | collective-permute-start | bytes 1572872 | tf_op jit(solution)/shard_map/ppermute | solution.py:27
  3.1 30.1 %collective-permute-start.16 = (bf16[4,64,1024]{2,1,0:T(8,128)(2,1)S(1)}, bf16[4,64,1024]{2,1,0:T(8,128)(2,1)S(1)}, u32[]{:S(2)}, u32[]{:S(2)}) collective-permute-start(bf16[4,64,1024]{2,1,0:T(8,128)(2,1)S(1)} %get-tuple-element.33.b0), channel_id=1, source_target_pairs={{16,0},{24,8},{0,16},{8,24},{48,32},{56,40},{32,48},{40,56},{80,64... | collective-permute-start | bytes 1572872 | tf_op jit(solution)/shard_map/ppermute | solution.py:27
  4.2 31.2 %collective-permute-start.17 = (bf16[4,64,1024]{2,1,0:T(8,128)(2,1)S(1)}, bf16[4,64,1024]{2,1,0:T(8,128)(2,1)}, u32[]{:S(2)}, u32[]{:S(2)}) collective-permute-start(bf16[4,64,1024]{2,1,0:T(8,128)(2,1)S(1)} %get-tuple-element.33.b0), channel_id=1, source_target_pairs={{24,0},{0,8},{8,16},{16,24},{56,32},{32,40},{40,48},{48,56},{88,64... | collective-permute-start | bytes 1572872 | tf_op jit(solution)/shard_map/ppermute | solution.py:27
  6.3 31.6 %collective-permute-start.25 = (bf16[4,64,1024]{2,1,0:T(8,128)(2,1)}, bf16[4,64,1024]{2,1,0:T(8,128)(2,1)}, u32[]{:S(2)}, u32[]{:S(2)}) collective-permute-start(bf16[4,64,1024]{2,1,0:T(8,128)(2,1)} %get-tuple-element.34.b0), channel_id=1, source_target_pairs={{32,0},{40,8},{48,16},{56,24},{64,32},{72,40},{80,48},{88,56},{96,... | collective-permute-start | bytes 1572872 | tf_op jit(solution)/shard_map/ppermute | solution.py:27
  9.3 22.9 %copy-start.11 = (bf16[528,128]{1,0:T(8,128)(2,1)}, bf16[528,128]{1,0:T(8,128)(2,1)S(1)}, u32[]{:S(2)}) copy-start(bf16[528,128]{1,0:T(8,128)(2,1)S(1)} %maximum_maximum_fusion.refs_2_) | copy-start | bytes 405508
  9.4 22.5 %collective-permute-start = (bf16[528,128]{1,0:T(8,128)(2,1)S(1)}, bf16[528,128]{1,0:T(8,128)(2,1)S(1)}, u32[]{:S(2)}, u32[]{:S(2)}) collective-permute-start(bf16[528,128]{1,0:T(8,128)(2,1)S(1)} %maximum_maximum_fusion.refs_2_), channel_id=1, source_target_pairs={{0,8},{8,16},{16,24},{24,32},{32,40},{40,48},{48,56},{56,64},{64,7... | collective-permute-start | bytes 405512 | tf_op jit(solution)/shard_map/ppermute | solution.py:326
  31.9 67.1 %copy-start.21 = (bf16[528,128]{1,0:T(8,128)(2,1)}, bf16[528,128]{1,0:T(8,128)(2,1)S(1)}, u32[]{:S(2)}) copy-start(bf16[528,128]{1,0:T(8,128)(2,1)S(1)} %collective-permute-done.refs_3_) | copy-start | bytes 405508
  31.9 16.7 %collective-permute-start.26 = (bf16[4,64,1024]{2,1,0:T(8,128)(2,1)}, bf16[4,64,1024]{2,1,0:T(8,128)(2,1)}, u32[]{:S(2)}, u32[]{:S(2)}) collective-permute-start(bf16[4,64,1024]{2,1,0:T(8,128)(2,1)} %get-tuple-element.34.b0), channel_id=1, source_target_pairs={{64,0},{72,8},{80,16},{88,24},{96,32},{104,40},{112,48},{120,56},{... | collective-permute-start | bytes 1572872 | tf_op jit(solution)/shard_map/ppermute | solution.py:27
  32.3 101.5 %copy-start.5 = (bf16[2,1040,128]{2,1,0:T(8,128)(2,1)}, bf16[2,1040,128]{2,1,0:T(8,128)(2,1)S(1)}, u32[]{:S(2)}) copy-start(bf16[2,1040,128]{2,1,0:T(8,128)(2,1)S(1)} %pad_maximum_fusion.4.refs_4_) | copy-start | bytes 1597444
  32.3 135.5 %collective-permute-start.1 = (bf16[2,1040,128]{2,1,0:T(8,128)(2,1)S(1)}, bf16[2,1040,128]{2,1,0:T(8,128)(2,1)S(1)}, u32[]{:S(2)}, u32[]{:S(2)}) collective-permute-start(bf16[2,1040,128]{2,1,0:T(8,128)(2,1)S(1)} %pad_maximum_fusion.4.refs_4_), channel_id=1, source_target_pairs={{8,0},{16,8},{24,16},{0,24},{40,32},{48,40},{56,48},{32,56},{72,64... | collective-permute-start | bytes 1597448 | tf_op jit(solution)/shard_map/ppermute | solution.py:27
  33.2 2.2 copy-start.13
  33.2 100.7 %collective-permute-start.27 = (bf16[4,64,1024]{2,1,0:T(8,128)(2,1)}, bf16[4,64,1024]{2,1,0:T(8,128)(2,1)}, u32[]{:S(2)}, u32[]{:S(2)}) collective-permute-start(bf16[4,64,1024]{2,1,0:T(8,128)(2,1)} %get-tuple-element.34.b0), channel_id=1, source_target_pairs={{96,0},{104,8},{112,16},{120,24},{0,32},{8,40},{16,48},{24,56},{32... | collective-permute-start | bytes 1572872 | tf_op jit(solution)/shard_map/ppermute | solution.py:27
  35.4 134.6 %collective-permute-start.6 = (bf16[2,1040,128]{2,1,0:T(8,128)(2,1)S(1)}, bf16[2,1040,128]{2,1,0:T(8,128)(2,1)S(1)}, u32[]{:S(2)}, u32[]{:S(2)}) collective-permute-start(bf16[2,1040,128]{2,1,0:T(8,128)(2,1)S(1)} %pad_maximum_fusion.4.refs_4_), channel_id=1, source_target_pairs={{24,0},{0,8},{8,16},{16,24},{56,32},{32,40},{40,48},{48,56},{88,64... | collective-permute-start | bytes 1597448 | tf_op jit(solution)/shard_map/ppermute | solution.py:27
  37.9 133.2 %collective-permute-start.2 = (bf16[2,1040,128]{2,1,0:T(8,128)(2,1)S(1)}, bf16[2,1040,128]{2,1,0:T(8,128)(2,1)S(1)}, u32[]{:S(2)}, u32[]{:S(2)}) collective-permute-start(bf16[2,1040,128]{2,1,0:T(8,128)(2,1)S(1)} %pad_maximum_fusion.4.refs_4_), channel_id=1, source_target_pairs={{32,0},{40,8},{48,16},{56,24},{64,32},{72,40},{80,48},{88,56},{96,... | collective-permute-start | bytes 1597448 | tf_op jit(solution)/shard_map/ppermute | solution.py:27
  48.6 125.1 %collective-permute-start.3 = (bf16[2,1040,128]{2,1,0:T(8,128)(2,1)S(1)}, bf16[2,1040,128]{2,1,0:T(8,128)(2,1)}, u32[]{:S(2)}, u32[]{:S(2)}) collective-permute-start(bf16[2,1040,128]{2,1,0:T(8,128)(2,1)S(1)} %pad_maximum_fusion.4.refs_4_), channel_id=1, source_target_pairs={{96,0},{104,8},{112,16},{120,24},{0,32},{8,40},{16,48},{24,56},{32... | collective-permute-start | bytes 1597448 | tf_op jit(solution)/shard_map/ppermute | solution.py:27
  133.9 43.8 %collective-permute-start.18 = (bf16[2,64,1024]{2,1,0:T(8,128)(2,1)}, bf16[2,64,1024]{2,1,0:T(8,128)(2,1)}, u32[]{:S(2)}, u32[]{:S(2)}) collective-permute-start(bf16[2,64,1024]{2,1,0:T(8,128)(2,1)} %get-tuple-element.17), channel_id=1, source_target_pairs={{96,0},{104,8},{112,16},{120,24},{0,32},{8,40},{16,48},{24,56},{32... | collective-permute-start | bytes 786440 | tf_op jit(solution)/shard_map/ppermute | solution.py:27
  167.8 8.3 %copy-start.6 = (bf16[2,1040,128]{2,1,0:T(8,128)(2,1)}, bf16[2,1040,128]{2,1,0:T(8,128)(2,1)S(1)}, u32[]{:S(2)}) copy-start(bf16[2,1040,128]{2,1,0:T(8,128)(2,1)S(1)} %collective-permute-done.1.refs_5_) | copy-start | bytes 1597444
  167.8 10.5 %collective-permute-start.19 = (bf16[2,64,1024]{2,1,0:T(8,128)(2,1)}, bf16[2,64,1024]{2,1,0:T(8,128)(2,1)}, u32[]{:S(2)}, u32[]{:S(2)}) collective-permute-start(bf16[2,64,1024]{2,1,0:T(8,128)(2,1)} %get-tuple-element.18), channel_id=1, source_target_pairs={{64,0},{72,8},{80,16},{88,24},{96,32},{104,40},{112,48},{120,56},{... | collective-permute-start | bytes 786440 | tf_op jit(solution)/shard_map/ppermute | solution.py:27
  170.0 6.2 %copy-start.7 = (bf16[2,1040,128]{2,1,0:T(8,128)(2,1)}, bf16[2,1040,128]{2,1,0:T(8,128)(2,1)S(1)}, u32[]{:S(2)}) copy-start(bf16[2,1040,128]{2,1,0:T(8,128)(2,1)S(1)} %collective-permute-done.6.refs_6_) | copy-start | bytes 1597444
  170.0 11.0 %collective-permute-start.20 = (bf16[2,64,1024]{2,1,0:T(8,128)(2,1)}, bf16[2,64,1024]{2,1,0:T(8,128)(2,1)}, u32[]{:S(2)}, u32[]{:S(2)}) collective-permute-start(bf16[2,64,1024]{2,1,0:T(8,128)(2,1)} %get-tuple-element.19), channel_id=1, source_target_pairs={{32,0},{40,8},{48,16},{56,24},{64,32},{72,40},{80,48},{88,56},{96,... | collective-permute-start | bytes 786440 | tf_op jit(solution)/shard_map/ppermute | solution.py:27
  171.1 5.0 %copy-start.8 = (bf16[2,1040,128]{2,1,0:T(8,128)(2,1)}, bf16[2,1040,128]{2,1,0:T(8,128)(2,1)S(1)}, u32[]{:S(2)}) copy-start(bf16[2,1040,128]{2,1,0:T(8,128)(2,1)S(1)} %collective-permute-done.2.refs_7_) | copy-start | bytes 1597444
  171.2 16.8 %collective-permute-start.28 = (bf16[2,64,1024]{2,1,0:T(8,128)(2,1)}, bf16[2,64,1024]{2,1,0:T(8,128)(2,1)S(1)}, u32[]{:S(2)}, u32[]{:S(2)}) collective-permute-start(bf16[2,64,1024]{2,1,0:T(8,128)(2,1)} %get-tuple-element.21), channel_id=1, source_target_pairs={{24,0},{0,8},{8,16},{16,24},{56,32},{32,40},{40,48},{48,56},{88,64... | collective-permute-start | bytes 786440 | tf_op jit(solution)/shard_map/ppermute | solution.py:27
  173.7 18.3 %collective-permute-start.29 = (bf16[2,64,1024]{2,1,0:T(8,128)(2,1)}, bf16[2,64,1024]{2,1,0:T(8,128)(2,1)S(1)}, u32[]{:S(2)}, u32[]{:S(2)}) collective-permute-start(bf16[2,64,1024]{2,1,0:T(8,128)(2,1)} %get-tuple-element.22), channel_id=1, source_target_pairs={{16,0},{24,8},{0,16},{8,24},{48,32},{56,40},{32,48},{40,56},{80,64... | collective-permute-start | bytes 786440 | tf_op jit(solution)/shard_map/ppermute | solution.py:27
  176.1 1.6 copy-start.25
  176.2 4.8 %copy-start.20 = (bf16[2,64,1024]{2,1,0:T(8,128)(2,1)S(1)}, bf16[2,64,1024]{2,1,0:T(8,128)(2,1)}, u32[]{:S(2)}) copy-start(bf16[2,64,1024]{2,1,0:T(8,128)(2,1)} %get-tuple-element.20) | copy-start | bytes 786436
  177.7 15.6 %copy-start.19 = (bf16[2,64,1024]{2,1,0:T(8,128)(2,1)S(1)}, bf16[2,64,1024]{2,1,0:T(8,128)(2,1)}, u32[]{:S(2)}) copy-start(bf16[2,64,1024]{2,1,0:T(8,128)(2,1)} %get-tuple-element.24) | copy-start | bytes 786436
  177.7 14.3 %collective-permute-start.30 = (bf16[2,64,1024]{2,1,0:T(8,128)(2,1)S(1)}, bf16[2,64,1024]{2,1,0:T(8,128)(2,1)S(1)}, u32[]{:S(2)}, u32[]{:S(2)}) collective-permute-start(bf16[2,64,1024]{2,1,0:T(8,128)(2,1)S(1)} %copy-done.25), channel_id=1, source_target_pairs={{8,0},{16,8},{24,16},{0,24},{40,32},{48,40},{56,48},{32,56},{72,64... | collective-permute-start | bytes 786440 | tf_op jit(solution)/shard_map/ppermute | solution.py:27
  178.4 49.3 %collective-permute-start.4 = (bf16[3,1040,128]{2,1,0:T(8,128)(2,1)S(1)}, bf16[3,1040,128]{2,1,0:T(8,128)(2,1)S(1)}, u32[]{:S(2)}, u32[]{:S(2)}) collective-permute-start(bf16[3,1040,128]{2,1,0:T(8,128)(2,1)S(1)} %get-tuple-element.38), channel_id=1, source_target_pairs={{8,0},{16,8},{24,16},{0,24},{40,32},{48,40},{56,48},{32,56},{72,64... | collective-permute-start | bytes 2396168 | tf_op jit(solution)/shard_map/ppermute | solution.py:27
  181.0 17.5 %copy-start.14 = (bf16[256,1024]{1,0:T(8,128)(2,1)S(1)}, bf16[256,1024]{1,0:T(8,128)(2,1)}, u32[]{:S(2)}) copy-start(bf16[256,1024]{1,0:T(8,128)(2,1)} %param.12) | copy-start | bytes 1572868
  182.7 1.9 collective-permute-start.21
  184.6 43.2 %collective-permute-start.7 = (bf16[3,1040,128]{2,1,0:T(8,128)(2,1)}, bf16[3,1040,128]{2,1,0:T(8,128)(2,1)S(1)}, u32[]{:S(2)}, u32[]{:S(2)}) collective-permute-start(bf16[3,1040,128]{2,1,0:T(8,128)(2,1)} %get-tuple-element.48), channel_id=1, source_target_pairs={{24,0},{0,8},{8,16},{16,24},{56,32},{32,40},{40,48},{48,56},{88,64... | collective-permute-start | bytes 2396168 | tf_op jit(solution)/shard_map/ppermute | solution.py:27
  187.9 5.7 %collective-permute-start.22 = (bf16[128,128]{0,1:T(8,128)(2,1)S(1)}, bf16[128,128]{0,1:T(8,128)(2,1)S(1)}, u32[]{:S(2)}, u32[]{:S(2)}) collective-permute-start(bf16[128,128]{0,1:T(8,128)(2,1)S(1)} %add_convert_fusion.1), channel_id=1, source_target_pairs={{2,0},{3,1},{4,2},{5,3},{6,4},{7,5},{0,6},{1,7},{10,8},{11,9},{12,... | collective-permute-start | bytes 98312 | tf_op jit(solution)/shard_map/ppermute | solution.py:35
  192.1 5.5 %collective-permute-start.23 = (bf16[128,128]{0,1:T(8,128)(2,1)S(1)}, bf16[128,128]{0,1:T(8,128)(2,1)S(1)}, u32[]{:S(2)}, u32[]{:S(2)}) collective-permute-start(bf16[128,128]{0,1:T(8,128)(2,1)S(1)} %add_convert_fusion.1), channel_id=1, source_target_pairs={{4,0},{5,1},{6,2},{7,3},{0,4},{1,5},{2,6},{3,7},{12,8},{13,9},{14,... | collective-permute-start | bytes 98312 | tf_op jit(solution)/shard_map/ppermute | solution.py:35
  192.1 6.3 %collective-permute-start.24 = (bf16[128,128]{0,1:T(8,128)(2,1)S(1)}, bf16[128,128]{0,1:T(8,128)(2,1)S(1)}, u32[]{:S(2)}, u32[]{:S(2)}) collective-permute-start(bf16[128,128]{0,1:T(8,128)(2,1)S(1)} %add_convert_fusion.1), channel_id=1, source_target_pairs={{6,0},{7,1},{0,2},{1,3},{2,4},{3,5},{4,6},{5,7},{14,8},{15,9},{8,1... | collective-permute-start | bytes 98312 | tf_op jit(solution)/shard_map/ppermute | solution.py:35
  193.7 37.1 %collective-permute-start.9 = (bf16[3,1040,128]{2,1,0:T(8,128)(2,1)}, bf16[3,1040,128]{2,1,0:T(8,128)(2,1)S(1)}, u32[]{:S(2)}, u32[]{:S(2)}) collective-permute-start(bf16[3,1040,128]{2,1,0:T(8,128)(2,1)} %get-tuple-element.47), channel_id=1, source_target_pairs={{32,0},{40,8},{48,16},{56,24},{64,32},{72,40},{80,48},{88,56},{96,... | collective-permute-start | bytes 2396168 | tf_op jit(solution)/shard_map/ppermute | solution.py:27
  197.5 31.2 %collective-permute-start.11 = (bf16[3,1040,128]{2,1,0:T(8,128)(2,1)}, bf16[3,1040,128]{2,1,0:T(8,128)(2,1)}, u32[]{:S(2)}, u32[]{:S(2)}) collective-permute-start(bf16[3,1040,128]{2,1,0:T(8,128)(2,1)} %get-tuple-element.37), channel_id=1, source_target_pairs={{96,0},{104,8},{112,16},{120,24},{0,32},{8,40},{16,48},{24,56},{32... | collective-permute-start | bytes 2396168 | tf_op jit(solution)/shard_map/ppermute | solution.py:27
  227.6 7.1 %copy-start.2 = (bf16[3,1040,128]{2,1,0:T(8,128)(2,1)}, bf16[3,1040,128]{2,1,0:T(8,128)(2,1)S(1)}, u32[]{:S(2)}) copy-start(bf16[3,1040,128]{2,1,0:T(8,128)(2,1)S(1)} %collective-permute-done.4.refs_4_) | copy-start | bytes 2396164
  227.7 6.9 %copy-start.3 = (bf16[3,1040,128]{2,1,0:T(8,128)(2,1)}, bf16[3,1040,128]{2,1,0:T(8,128)(2,1)S(1)}, u32[]{:S(2)}) copy-start(bf16[3,1040,128]{2,1,0:T(8,128)(2,1)S(1)} %collective-permute-done.7.refs_5_) | copy-start | bytes 2396164
  228.7 38.1 %collective-permute-start.8 = (bf16[2,1040,128]{2,1,0:T(8,128)(2,1)}, bf16[2,1040,128]{2,1,0:T(8,128)(2,1)S(1)}, u32[]{:S(2)}, u32[]{:S(2)}) collective-permute-start(bf16[2,1040,128]{2,1,0:T(8,128)(2,1)} %slice.263), channel_id=1, source_target_pairs={{24,0},{0,8},{8,16},{16,24},{56,32},{32,40},{40,48},{48,56},{88,64... | collective-permute-start | bytes 1597448 | tf_op jit(solution)/shard_map/ppermute | solution.py:27
  230.6 36.4 %collective-permute-start.12 = (bf16[2,1040,128]{2,1,0:T(8,128)(2,1)}, bf16[2,1040,128]{2,1,0:T(8,128)(2,1)}, u32[]{:S(2)}, u32[]{:S(2)}) collective-permute-start(bf16[2,1040,128]{2,1,0:T(8,128)(2,1)} %slice.269), channel_id=1, source_target_pairs={{96,0},{104,8},{112,16},{120,24},{0,32},{8,40},{16,48},{24,56},{32... | collective-permute-start | bytes 1597448 | tf_op jit(solution)/shard_map/ppermute | solution.py:27
  230.7 8.0 %copy-start.4 = (bf16[3,1040,128]{2,1,0:T(8,128)(2,1)}, bf16[3,1040,128]{2,1,0:T(8,128)(2,1)S(1)}, u32[]{:S(2)}) copy-start(bf16[3,1040,128]{2,1,0:T(8,128)(2,1)S(1)} %collective-permute-done.9.refs_6_) | copy-start | bytes 2396164
  231.8 37.0 %collective-permute-start.5 = (bf16[2,1040,128]{2,1,0:T(8,128)(2,1)}, bf16[2,1040,128]{2,1,0:T(8,128)(2,1)}, u32[]{:S(2)}, u32[]{:S(2)}) collective-permute-start(bf16[2,1040,128]{2,1,0:T(8,128)(2,1)} %slice.258), channel_id=1, source_target_pairs={{8,0},{16,8},{24,16},{0,24},{40,32},{48,40},{56,48},{32,56},{72,64... | collective-permute-start | bytes 1597448 | tf_op jit(solution)/shard_map/ppermute | solution.py:27
  234.7 34.8 %collective-permute-start.10 = (bf16[2,1040,128]{2,1,0:T(8,128)(2,1)S(1)}, bf16[2,1040,128]{2,1,0:T(8,128)(2,1)S(1)}, u32[]{:S(2)}, u32[]{:S(2)}) collective-permute-start(bf16[2,1040,128]{2,1,0:T(8,128)(2,1)S(1)} %slice.267), channel_id=1, source_target_pairs={{32,0},{40,8},{48,16},{56,24},{64,32},{72,40},{80,48},{88,56},{96,... | collective-permute-start | bytes 1597448 | tf_op jit(solution)/shard_map/ppermute | solution.py:27
  266.8 9.6 %copy-start.10 = (bf16[2,1040,128]{2,1,0:T(8,128)(2,1)}, bf16[2,1040,128]{2,1,0:T(8,128)(2,1)S(1)}, u32[]{:S(2)}) copy-start(bf16[2,1040,128]{2,1,0:T(8,128)(2,1)S(1)} %collective-permute-done.8.refs_5_) | copy-start | bytes 1597444
  266.9 6.5 %collective-permute-start.14 = (bf16[1,1040,128]{2,1,0:T(8,128)(2,1)S(1)}, bf16[1,1040,128]{2,1,0:T(8,128)(2,1)S(1)}, u32[]{:S(2)}, u32[]{:S(2)}) collective-permute-start(bf16[1,1040,128]{2,1,0:T(8,128)(2,1)S(1)} %slice.273), channel_id=1, source_target_pairs={{32,0},{40,8},{48,16},{56,24},{64,32},{72,40},{80,48},{88,56},{96,... | collective-permute-start | bytes 798728 | tf_op jit(solution)/shard_map/ppermute | solution.py:27
  268.0 7.7 %collective-permute-start.13 = (bf16[1,1040,128]{2,1,0:T(8,128)(2,1)S(1)}, bf16[1,1040,128]{2,1,0:T(8,128)(2,1)S(1)}, u32[]{:S(2)}, u32[]{:S(2)}) collective-permute-start(bf16[1,1040,128]{2,1,0:T(8,128)(2,1)S(1)} %slice.271), channel_id=1, source_target_pairs={{8,0},{16,8},{24,16},{0,24},{40,32},{48,40},{56,48},{32,56},{72,64... | collective-permute-start | bytes 798728 | tf_op jit(solution)/shard_map/ppermute | solution.py:27
  269.5 0.8 copy-start.12
  273.4 3.1 %copy-start.15 = (bf16[1,1040,128]{2,1,0:T(8,128)(2,1)}, bf16[1,1040,128]{2,1,0:T(8,128)(2,1)S(1)}, u32[]{:S(2)}) copy-start(bf16[1,1040,128]{2,1,0:T(8,128)(2,1)S(1)} %collective-permute-done.14.refs_9_) | copy-start | bytes 798724
  275.7 0.7 copy-start.16

commit v2 on v0

v2 whole, which is shorter than its diff:
```python
import functools
import math

import jax
import jax.numpy as jnp
from jax import lax
from jax.experimental import pallas as pl
from jax.experimental.pallas import tpu as pltpu
from jax.sharding import PartitionSpec as P

HEAD_SIZE = 128
PAGE = 128
SIDE = 4
RANK = 64
HEADS = 8
TILE = 64
GROUP = 8
STEP_ROWS = TILE * HEADS
NEG = -1e30
VMEM_LIMIT = 56 * 1024 * 1024
LOG_SCALE = math.log2(math.e) / math.sqrt(HEAD_SIZE)

adapter_scale = 2.0


def pull(block, dx, dy):
    route = []
    for i in range(SIDE * SIDE):
        y, x = divmod(i, SIDE)
        route.append((((y + dy) % SIDE) * SIDE + (x + dx) % SIDE, i))
    return lax.ppermute(block, "ctx", route)


def pull_tp(block, dz, dc):
    route = []
    for i in range(2 * SIDE):
        z, c = divmod(i, 2)
        route.append((((z + dz) % SIDE) * 2 + (c ^ dc), i))
    return lax.ppermute(block, "tp", route)


def stored_row(slot_ref, segment_ref, segment):
    return slot_ref[segment_ref[segment]]


def place(index, along_x):
    y, x = index // SIDE, lax.rem(index, SIDE)
    return (x, y) if along_x else (y, x)


def pick_kernel(meta_ref, slot_ref, segment_ref, *refs):
    bufs, outs, sems = refs[0:8], refs[8:16], refs[16]
    me = meta_ref[0]
    for f, along_x in enumerate((True, False)):
        along, across = place(me, along_x)
        for d in range(SIDE):
            there = lax.rem(across + d, SIDE)
            dest = there * SIDE + along if along_x else along * SIDE + there
            for k in range(2):
                row = stored_row(slot_ref, segment_ref, dest + k)
                owner_along, _ = place(row // 4, along_x)
                ring = lax.rem(owner_along - along + SIDE, SIDE)
                for b in range(SIDE):
                    @pl.when(ring == b)
                    def _():
                        pltpu.make_async_copy(
                            bufs[f * 4 + b].at[lax.rem(row, 4)],
                            outs[f * 4 + d].at[k],
                            sems.at[f * 8 + d * 2 + k],
                        ).start()
    for f in range(2):
        for d in range(SIDE):
            for k in range(2):
                pltpu.make_async_copy(
                    bufs[f * 4].at[0], outs[f * 4 + d].at[k], sems.at[f * 8 + d * 2 + k]
                ).wait()


def pick(meta, slot, segment, bufs):
    out = jax.ShapeDtypeStruct((2,) + bufs[0].shape[1:], jnp.bfloat16)
    smem = pl.BlockSpec(memory_space=pltpu.SMEM)
    return pl.pallas_call(
        pick_kernel,
        out_shape=[out] * 8,
        in_specs=[smem] * 3 + [pl.BlockSpec(memory_space=pl.ANY)] * 8,
        out_specs=[pl.BlockSpec(memory_space=pltpu.VMEM)] * 8,
        scratch_shapes=[pltpu.SemaphoreType.DMA((16,))],
        name="pick_items",
    )(meta, slot, segment, *bufs)


def ring_rows(raw_x, raw_y):
    return [
        raw_x, pull(raw_x, 1, 0), pull(raw_x, 2, 0), pull(raw_x, -1, 0),
        raw_y, pull(raw_y, 0, 1), pull(raw_y, 0, 2), pull(raw_y, 0, -1),
    ]


def hand_over(items):
    return [
        items[0], pull(items[3], 0, 1), pull(items[2], 0, 2), pull(items[1], 0, -1),
        items[4], pull(items[7], 1, 0), pull(items[6], 2, 0), pull(items[5], -1, 0),
    ]


def keep_items(meta_ref, slot_ref, segment_ref, got, store):
    me = meta_ref[0]
    for f, along_x in enumerate((True, False)):
        _, across = place(me, along_x)
        for k in range(2):
            row = stored_row(slot_ref, segment_ref, me + k)
            _, owner_across = place(row // 4, along_x)
            source = lax.rem(owner_across - across + SIDE, SIDE)
            for d in range(SIDE):
                @pl.when(source == d)
                def _():
                    store(k, f * (RANK // 2), got[f * 4 + d][k])


def rank_kernel(meta_ref, slot_ref, segment_ref, tokens_ref, *refs):
    got, out_ref, down, swapped = refs[0:8], refs[8], refs[9], refs[10]

    def store(k, offset, block):
        part = block[:RANK // 2]
        down[k * RANK + offset:k * RANK + offset + RANK // 2, :] = part
        other = (1 - k) * RANK + offset
        swapped[other:other + RANK // 2, :] = part

    keep_items(meta_ref, slot_ref, segment_ref, got, store)
    cut = meta_ref[1]
    half = out_ref.shape[0]
    dims = (((1,), (1,)), ((), ()))
    tokens = tokens_ref[...]
    straight = lax.dot_general(tokens, down[...], dims, preferred_element_type=jnp.float32)
    crossed = lax.dot_general(tokens, swapped[...], dims, preferred_element_type=jnp.float32)
    row = lax.broadcasted_iota(jnp.int32, (half, 2 * RANK), 0)
    lane = lax.broadcasted_iota(jnp.int32, (half, 2 * RANK), 1)
    top = jnp.where(row < cut, straight[:half], crossed[:half])
    bottom = jnp.where(row + half < cut, crossed[half:], straight[half:])
    out_ref[...] = jnp.where(lane < RANK, top, bottom).astype(jnp.bfloat16)


def rank_part(meta, slot, segment, tokens, got):
    smem = pl.BlockSpec(memory_space=pltpu.SMEM)
    vmem = pl.BlockSpec(memory_space=pltpu.VMEM)
    rows, width = tokens.shape
    return pl.pallas_call(
        rank_kernel,
        out_shape=jax.ShapeDtypeStruct((rows // 2, 2 * RANK), jnp.bfloat16),
        in_specs=[smem] * 3 + [vmem] * 9,
        out_specs=vmem,
        scratch_shapes=[pltpu.VMEM((2 * RANK, width), jnp.bfloat16)] * 2,
        name="rank_part",
    )(meta, slot, segment, tokens, *got)


def query_kernel(meta_ref, slot_ref, segment_ref, base_ref, *refs):
    parts, got, q_ref, up = refs[0:8], refs[8:16], refs[16], refs[17]

    def store(k, offset, block):
        for start in ((k * RANK), (3 - k) * RANK):
            up[start + offset:start + offset + RANK // 2, :] = block[RANK // 2:]

    keep_items(meta_ref, slot_ref, segment_ref, got, store)
    cut = meta_ref[1]
    total = functools.reduce(jnp.add, [p[...].astype(jnp.float32) for p in parts])
    half = total.shape[0]
    row = lax.broadcasted_iota(jnp.int32, (half, 2 * RANK), 0)
    lane = lax.broadcasted_iota(jnp.int32, (half, 2 * RANK), 1)
    left = lane < RANK
    zero = jnp.zeros_like(total)

    def masked(keep):
        return jnp.where(keep, total, zero).astype(jnp.bfloat16)

    first, second = row < cut, row + half < cut
    lhs = jnp.concatenate(
        [
            jnp.concatenate([masked(left & first), masked(left & ~first)], axis=1),
            jnp.concatenate([masked(~left & ~second), masked(~left & second)], axis=1),
        ],
        axis=0,
    )
    tiles = 2 * half // TILE
    for t in range(tiles):
        rows = slice(t * TILE, (t + 1) * TILE)
        lora = jnp.dot(lhs[rows], up[...], preferred_element_type=jnp.float32)
        q = (base_ref[rows, :].astype(jnp.float32) + adapter_scale * lora).astype(jnp.bfloat16)
        for h in range(HEADS):
            at = (t * HEADS + h) * TILE
            q_ref[at:at + TILE, :] = q[:, h * HEAD_SIZE:(h + 1) * HEAD_SIZE]
    mixed = jnp.minimum(cut // TILE, tiles - 1)
    q_ref[tiles * STEP_ROWS:(tiles + 1) * STEP_ROWS, :] = q_ref[
        pl.ds(pl.multiple_of(mixed * STEP_ROWS, STEP_ROWS), STEP_ROWS), :
    ]


def queries(meta, slot, segment, base, parts, got):
    smem = pl.BlockSpec(memory_space=pltpu.SMEM)
    vmem = pl.BlockSpec(memory_space=pltpu.VMEM)
    rows, width = base.shape
    return pl.pallas_call(
        query_kernel,
        out_shape=jax.ShapeDtypeStruct((rows * HEADS + STEP_ROWS, HEAD_SIZE), jnp.bfloat16),
        in_specs=[smem] * 3 + [vmem] * 17,
        out_specs=vmem,
        scratch_shapes=[pltpu.VMEM((4 * RANK, width), jnp.bfloat16)],
        compiler_params=pltpu.CompilerParams(vmem_limit_bytes=VMEM_LIMIT),
        name="queries",
    )(meta, slot, segment, base, *parts, *got)


def attend_kernel(blocks, *refs):
    meta_ref, q_ref, span_ref, prev_ref, cache_ref, out_ref = refs[:6]
    (k_sc, v_sc, count_sc, steps, m_sc, al_sc, s_even, s_odd,
     id_rows, id_vec, id_sc, id_sem, k_sem, v_sem) = refs[6:]
    rows_all = q_ref.shape[0] - STEP_ROWS
    tiles = rows_all // STEP_ROWS
    keys_step = GROUP * PAGE
    groups = k_sc.shape[0] // 2 // keys_step
    own_rows = cache_ref.shape[0] // blocks
    own_pages = (own_rows - 16) // (2 * PAGE)
    seg_a, cut, prev_cut = meta_ref[0], meta_ref[1], meta_ref[2]

    for d in range(blocks):
        pltpu.make_async_copy(
            cache_ref.at[pl.ds((d + 1) * own_rows - 16, 16)], id_rows.at[d], id_sem.at[d]
        ).start()

    def rows_at(start):
        return pl.ds(pl.multiple_of(start, STEP_ROWS), STEP_ROWS)

    def keys_at(g):
        return pl.ds(pl.multiple_of(g * keys_step, keys_step), keys_step)

    def score(i, s_ref):
        at = jnp.minimum(steps[2 * i], rows_all)
        s_ref[...] = lax.dot_general(
            q_ref[rows_at(at), :],
            k_sc[keys_at(steps[2 * i + 1]), :],
            (((1,), (1,)), ((), ())),
            preferred_element_type=jnp.float32,
        )

    def soften(i, s_ref):
        rows = rows_at(steps[2 * i])
        parts = [s_ref[:, j * 128:(j + 1) * 128] for j in range(GROUP)]
        peak = jnp.max(functools.reduce(jnp.maximum, parts), axis=1, keepdims=True) * LOG_SCALE
        old = m_sc[rows, :]
        new = jnp.maximum(old, peak)
        fade = jnp.exp2(old - new)
        weights = jnp.concatenate(
            [jnp.exp2(s * LOG_SCALE - new).astype(jnp.bfloat16) for s in parts], axis=1
        )
        added = jnp.dot(weights, v_sc[keys_at(steps[2 * i + 1]), :], preferred_element_type=jnp.float32)
        m_sc[rows, :] = new
        al_sc[rows, 0:128] = al_sc[rows, 0:128] * fade + added[:, 0:128]
        al_sc[rows, 128:256] = al_sc[rows, 128:256] * fade + added[:, 128:256]

    for d in range(blocks):
        pltpu.make_async_copy(
            cache_ref.at[pl.ds((d + 1) * own_rows - 16, 16)], id_rows.at[d], id_sem.at[d]
        ).wait()
    for d in range(blocks):
        id_vec[d:d + 1, :] = id_rows[d].astype(jnp.int32)[0:1, :]
    copy = pltpu.make_async_copy(id_vec, id_sc, id_sem.at[0])
    copy.start()
    copy.wait()

    count_sc[0] = 0
    count_sc[1] = 0

    def page_copies(d, page, slot):
        here = pl.ds(pl.multiple_of(slot * PAGE, PAGE), PAGE)
        at = pl.multiple_of(d * own_rows + page * PAGE, 16)
        keys = pltpu.make_async_copy(cache_ref.at[pl.ds(at, PAGE)], k_sc.at[here], k_sem)
        at = pl.multiple_of(d * own_rows + (own_pages + page) * PAGE, 16)
        values = pltpu.make_async_copy(
            cache_ref.at[pl.ds(at, PAGE)], v_sc.at[here, pl.ds(0, 128)], v_sem
        )
        return keys, values

    @pl.loop(0, blocks * own_pages)
    def _(i):
        d, page = i // own_pages, lax.rem(i, own_pages)
        which = id_sc[d, page] - seg_a

        @pl.when((which == 0) | (which == 1))
        def _():
            n = count_sc[which]
            for c in page_copies(d, page, which * groups * GROUP + n):
                c.start()
            count_sc[which] = n + 1

    span_keys = jnp.concatenate([prev_ref[0:256, :], span_ref[0:256, :]], axis=0)
    span_values = jnp.concatenate(
        [
            jnp.concatenate([prev_ref[256:512, :], span_ref[256:512, :]], axis=0),
            jnp.ones((512, 128), jnp.bfloat16),
        ],
        axis=1,
    )

    @pl.loop(0, tiles)
    def _(t):
        rows = rows_at(t * STEP_ROWS)
        scores = lax.dot_general(
            q_ref[rows, :], span_keys, (((1,), (1,)), ((), ())), preferred_element_type=jnp.float32
        )
        token = t * TILE + lax.broadcasted_iota(jnp.int32, (STEP_ROWS, 512), 0) % TILE
        key = lax.broadcasted_iota(jnp.int32, (STEP_ROWS, 512), 1) - 256
        in_a = token < cut
        keep = ((key < 0) & in_a & (key + 256 >= prev_cut)) | (
            (key >= 0) & (key <= token) & ((key < cut) == in_a)
        )
        scores = jnp.where(keep, scores * LOG_SCALE, NEG)
        peak = jnp.max(scores, axis=1, keepdims=True)
        weights = jnp.exp2(scores - peak).astype(jnp.bfloat16)
        m_sc[rows, :] = jnp.broadcast_to(peak, (STEP_ROWS, 128))
        al_sc[rows, :] = jnp.dot(weights, span_values, preferred_element_type=jnp.float32)

    mixed_start = jnp.minimum(cut // TILE, tiles - 1) * STEP_ROWS
    mixed = rows_at(mixed_start)
    m_sc[rows_all:rows_all + STEP_ROWS, :] = m_sc[mixed, :]
    al_sc[rows_all:rows_all + STEP_ROWS, :] = al_sc[mixed, :]

    @pl.loop(0, count_sc[0] + count_sc[1])
    def _(i):
        for c in page_copies(0, 0, 0):
            c.wait()

    count_sc[2] = 0
    for side in range(2):
        n = count_sc[side]
        full = (n + GROUP - 1) // GROUP
        base = side * groups * keys_step

        @pl.loop(0, n)
        def _(i, base=base):
            there = pl.ds(pl.multiple_of(base + i * PAGE, PAGE), PAGE)
            v_sc[there, 128:256] = jnp.ones((PAGE, 128), jnp.bfloat16)

        @pl.loop(n, full * GROUP)
        def _(i, base=base):
            there = pl.ds(pl.multiple_of(base + i * PAGE, PAGE), PAGE)
            k_sc[there, :] = k_sc[base:base + PAGE, :]
            v_sc[there, :] = jnp.zeros((PAGE, 256), jnp.bfloat16)

        low = 0 if side == 0 else cut // TILE
        high = (cut + TILE - 1) // TILE if side == 0 else tiles

        @pl.loop(0, full)
        def _(g, side=side, low=low, high=high):
            @pl.loop(low, high)
            def _(t):
                c = count_sc[2]
                start = t * STEP_ROWS
                if side == 1:
                    start = jnp.where(t == low, rows_all, start)
                steps[2 * c] = start
                steps[2 * c + 1] = side * groups + g
                count_sc[2] = c + 1

    total = count_sc[2]
    for e in range(2):
        steps[2 * (total + e)] = rows_all + STEP_ROWS
        steps[2 * (total + e) + 1] = 0

    @pl.when(total > 0)
    def _():
        score(0, s_even)

    @pl.loop(0, (total + 1) // 2)
    def _(j):
        score(2 * j + 1, s_odd)
        soften(2 * j, s_even)
        score(2 * j + 2, s_even)
        soften(2 * j + 1, s_odd)

    token = (mixed_start // STEP_ROWS) * TILE + (
        lax.broadcasted_iota(jnp.int32, (STEP_ROWS, 128), 0) % TILE
    )
    in_a = token < cut
    for c in range(2):
        cols = slice(c * 128, (c + 1) * 128)
        al_sc[mixed, cols] = jnp.where(
            in_a, al_sc[mixed, cols], al_sc[rows_all:rows_all + STEP_ROWS, cols]
        )
    for t in range(tiles):
        for h in range(HEADS):
            at = (t * HEADS + h) * TILE
            out = al_sc[at:at + TILE, 0:128] / al_sc[at:at + TILE, 128:256]
            out_ref[t * TILE:(t + 1) * TILE, h * 128:(h + 1) * 128] = out.astype(jnp.bfloat16)


def attend(meta, q, span, prev, cache, blocks):
    rows = q.shape[0] - STEP_ROWS
    tiles = rows // STEP_ROWS
    pages = (cache.shape[0] // blocks - 16) // (2 * PAGE) * blocks
    groups = -(-pages // GROUP)
    vmem = pl.BlockSpec(memory_space=pltpu.VMEM)
    id_shape = (-(-blocks // 8) * 8, 128)
    return pl.pallas_call(
        functools.partial(attend_kernel, blocks),
        out_shape=jax.ShapeDtypeStruct((rows // HEADS, HEADS * HEAD_SIZE), jnp.bfloat16),
        in_specs=[pl.BlockSpec(memory_space=pltpu.SMEM), vmem, vmem, vmem, pl.BlockSpec(memory_space=pl.ANY)],
        out_specs=vmem,
        scratch_shapes=[
            pltpu.VMEM((2 * groups * GROUP * PAGE, 128), jnp.bfloat16),
            pltpu.VMEM((2 * groups * GROUP * PAGE, 256), jnp.bfloat16),
            pltpu.SMEM((3,), jnp.int32),
            pltpu.SMEM((2 * ((tiles + 1) * groups + 4),), jnp.int32),
            pltpu.VMEM((rows + 2 * STEP_ROWS, 128), jnp.float32),
            pltpu.VMEM((rows + 2 * STEP_ROWS, 256), jnp.float32),
            pltpu.VMEM((STEP_ROWS, GROUP * PAGE), jnp.float32),
            pltpu.VMEM((STEP_ROWS, GROUP * PAGE), jnp.float32),
            pltpu.VMEM((blocks, 16, 128), jnp.bfloat16),
            pltpu.VMEM(id_shape, jnp.int32),
            pltpu.SMEM(id_shape, jnp.int32),
            pltpu.SemaphoreType.DMA((blocks,)),
            pltpu.SemaphoreType.DMA(()),
            pltpu.SemaphoreType.DMA(()),
        ],
        compiler_params=pltpu.CompilerParams(vmem_limit_bytes=VMEM_LIMIT),
        name="attend",
    )(meta, q, span, prev, cache)


def per_device(
    tokens_in,
    base_queries,
    fresh_keys,
    fresh_values,
    cached_key_rows,
    cached_value_rows,
    adapter_store,
    adapter_slot,
    segment_adapter,
    token_request,
    cache_doc,
):
    tok_rows = tokens_in.shape[0]
    me = lax.axis_index("ctx")
    seg_a = token_request[0]
    cut = jnp.sum((token_request == seg_a).astype(jnp.int32))
    meta = jnp.stack([seg_a, cut])
    ids = (meta, adapter_slot, segment_adapter)

    docs = jnp.pad(cache_doc, (0, 128 - cache_doc.shape[0])).astype(jnp.bfloat16)
    own = jnp.concatenate(
        [cached_key_rows, cached_value_rows, jnp.broadcast_to(docs[None], (16, 128))], axis=0
    )
    cache = lax.all_gather(own, "ctx", axis=0, tiled=True)

    mid = RANK // 2
    width = adapter_store.shape[3]
    rows = ring_rows(
        adapter_store[:, :, :mid].reshape(-1, RANK, width),
        adapter_store[:, :, mid:].reshape(-1, RANK, width),
    )
    got = hand_over(pick(*ids, rows))

    span = jnp.concatenate(
        [fresh_keys, fresh_values, jnp.broadcast_to(cut.astype(jnp.bfloat16), (16, 128))], axis=0
    )
    prev = lax.ppermute(span, "ctx", [(i - 1, i) for i in range(1, SIDE * SIDE)])
    prev_cut = jnp.where(me == 0, tok_rows, prev[512, 0].astype(jnp.int32))

    acts = rank_part(*ids, tokens_in, got)
    parts = [acts] + [pull_tp(acts, dz, dc) for dz in range(SIDE) for dc in range(2) if dz or dc]
    query = queries(*ids, base_queries, parts, got)
    info = jnp.concatenate([meta, prev_cut[None]])
    return attend(info, query, span, prev, cache, SIDE * SIDE)


def solution(mesh):
    in_specs = (
        P("ctx", "tp"),
        P("ctx", "tp"),
        P("ctx", "tp"),
        P("ctx", "tp"),
        P("ctx", "tp"),
        P("ctx", "tp"),
        P("ctx", None, None, "tp"),
        P(),
        P(),
        P("ctx"),
        P("ctx"),
    )
    out_specs = P("ctx", "tp")
    return jax.shard_map(
        per_device, mesh=mesh, in_specs=in_specs, out_specs=out_specs, check_vma=False
    )
```

time: 440 us -> 154 us (0.35)
  the two profiles are of different devices: /device:TPU:22 before, /device:TPU:25 now
where the time goes in v2:
time: 154 us
  Pallas kernels  46.8 us (30%)
  waiting for transfers between devices  44.5 us (29%)
  starting transfers between devices  36.4 us (24%)
  between operations  15 us (10%)
  other arithmetic  7.65 us (5%)
  local copies, waits for them, and re-layouts  3.7 us (2%)
    ppermute x12, waiting for transfers between devices, pull(): return lax.ppermute(block, 'ctx', route)  41.6 us
    pallas_call x1, Pallas kernels, attend(): pl.pallas_call(functools.partial(attend_kernel, blocks), out_shape=jax.Sh...  36.7 us
    ppermute x12, starting transfers between devices, pull(): return lax.ppermute(block, 'ctx', route)  18.5 us
    ppermute x7, starting transfers between devices, pull_tp(): return lax.ppermute(block, 'tp', route)  11.1 us
    ppermute x1, starting transfers between devices, per_device(): lax.ppermute(span, 'ctx', [(i - 1, i) for i in range(1, SIDE * SIDE)])  6.77 us
    pallas_call x1, Pallas kernels, pick(): pl.pallas_call(pick_kernel, out_shape=[out] * 8, in_specs=[smem] * 3 + [p...  3.8 us
    pallas_call x1, Pallas kernels, queries(): pl.pallas_call(query_kernel, out_shape=jax.ShapeDtypeStruct((rows * HEADS...  3.34 us
  transfers between devices with their start and end apart: 21, of which 6 were waited for; matrix products, arithmetic and copies ran while one was open for 4% of the time, Pallas kernels for 7%

profile of v2, /device:TPU:25, one launch (start us, length us, event | category | flops | bytes accessed | tf_op | source)
XLA Modules:
  0.0 153.9 jit_solution(3837878523356433033)
XLA Ops:
  6.5 0.7 convert.5
  7.3 1.9 %pad_maximum_fusion = bf16[2064,128]{1,0:T(8,128)(2,1)} fusion(bf16[16,128]{1,0:T(8,128)(2,1)S(1)} %broadcast_in_dim.14, bf16[1024,128]{1,0:T(8,128)(2,1)} %param.16, bf16[1024,128]{1,0:T(8,128)(2,1)} %param.15), kind=kLoop, calls=%fused_computation | loop fusion | flops 1585152 | bytes 1056768 | tf_op jit(solution)/shard_map/concatenate | solution.py:450
  9.2 0.0 all-gather.2.cloned.1.call-update
  9.2 0.0 copy-start.25
  9.2 0.1 fusion.1
  9.3 0.0 copy-start.1
  9.3 2.5 %collective-permute-start.1 = (bf16[4,64,1024]{2,1,0:T(8,128)(2,1)S(1)}, bf16[4,64,1024]{2,1,0:T(8,128)(2,1)S(1)}, u32[]{:S(2)}, u32[]{:S(2)}) collective-permute-start(bf16[4,64,1024]{2,1,0:T(8,128)(2,1)S(1)} %bitcast.11), channel_id=1, source_target_pairs={{8,0},{16,8},{24,16},{0,24},{40,32},{48,40},{56,48},{32,56},{72,64... | collective-permute-start | bytes 1572872 | tf_op jit(solution)/shard_map/ppermute | solution.py:31
  11.9 0.5 collective-permute-start.2
  12.4 0.6 collective-permute-start.3
  13.0 0.5 collective-permute-start.4
  13.5 0.7 collective-permute-start.5
  14.1 9.1 %collective-permute-done.1.refs_1_ = bf16[4,64,1024]{2,1,0:T(8,128)(2,1)S(1)} collective-permute-done((bf16[4,64,1024]{2,1,0:T(8,128)(2,1)S(1)}, bf16[4,64,1024]{2,1,0:T(8,128)(2,1)S(1)}, u32[]{:S(2)}, u32[]{:S(2)}) %collective-permute-start.1) | collective-permute-done | bytes 524320 | tf_op jit(solution)/shard_map/ppermute | solution.py:31
  23.3 1.5 collective-permute-start.6
  24.7 0.5 slice.12
  25.3 1.2 fusion
  26.5 1.8 %pad_add_fusion.1.meta_ref = s32[2]{0:T(128)} fusion(s32[1]{0:T(128)} %bitcast.1, s32[1]{0:T(128)} %slice.12), kind=kLoop, calls=%fused_computation.5 | loop fusion | flops 2 | bytes 16 | tf_op jit(solution)/shard_map/stack | solution.py:446
  28.3 0.0 collective-permute-done.2.refs_2_
  28.3 18.7 %collective-permute-done.3.refs_3_ = bf16[4,64,1024]{2,1,0:T(8,128)(2,1)S(1)} collective-permute-done((bf16[4,64,1024]{2,1,0:T(8,128)(2,1)S(1)}, bf16[4,64,1024]{2,1,0:T(8,128)(2,1)S(1)}, u32[]{:S(2)}, u32[]{:S(2)}) %collective-permute-start.3) | collective-permute-done | bytes 524320 | tf_op jit(solution)/shard_map/ppermute | solution.py:31
  47.1 0.0 collective-permute-done.4.refs_5_
  47.1 0.0 collective-permute-done.5.refs_6_
  47.1 0.9 copy-done.14
  47.9 0.0 collective-permute-done.6.refs_7_
  48.0 0.0 copy-done.10
  48.0 0.1 copy-done.12
  48.1 0.2 copy-done.13
  48.3 3.8 %pick_items.1 = (bf16[2,64,1024]{2,1,0:T(8,128)(2,1)}, bf16[2,64,1024]{2,1,0:T(8,128)(2,1)}, bf16[2,64,1024]{2,1,0:T(8,128)(2,1)}, bf16[2,64,1024]{2,1,0:T(8,128...) custom-call(s32[2]{0:T(128)} %pad_add_fusion.1.meta_ref, ...), custom_call_target="tpu_custom_call" | custom-call | tf_op jit(solution)/shard_map/pick_items/pallas_call | solution.py:82
  52.1 0.3 collective-permute-start.10
  52.4 2.1 %collective-permute-start.11 = (bf16[2,64,1024]{2,1,0:T(8,128)(2,1)}, bf16[2,64,1024]{2,1,0:T(8,128)(2,1)S(1)}, u32[]{:S(2)}, u32[]{:S(2)}) collective-permute-start(bf16[2,64,1024]{2,1,0:T(8,128)(2,1)} %get-tuple-element.19), channel_id=1, source_target_pairs={{16,0},{24,8},{0,16},{8,24},{48,32},{56,40},{32,48},{40,56},{80,64... | collective-permute-start | bytes 786440 | tf_op jit(solution)/shard_map/ppermute | solution.py:31
  55.1 0.1 collective-permute-start.12
  55.2 1.5 collective-permute-start.7
  56.7 3.3 %collective-permute-start.8 = (bf16[2,64,1024]{2,1,0:T(8,128)(2,1)}, bf16[2,64,1024]{2,1,0:T(8,128)(2,1)S(1)}, u32[]{:S(2)}, u32[]{:S(2)}) collective-permute-start(bf16[2,64,1024]{2,1,0:T(8,128)(2,1)} %get-tuple-element.15), channel_id=1, source_target_pairs={{64,0},{72,8},{80,16},{88,24},{96,32},{104,40},{112,48},{120,56},{... | collective-permute-start | bytes 786440 | tf_op jit(solution)/shard_map/ppermute | solution.py:31
  60.0 0.0 collective-permute-done.10.refs_5_.refs_13_
  60.0 5.0 %collective-permute-start.9 = (bf16[2,64,1024]{2,1,0:T(8,128)(2,1)}, bf16[2,64,1024]{2,1,0:T(8,128)(2,1)S(1)}, u32[]{:S(2)}, u32[]{:S(2)}) collective-permute-start(bf16[2,64,1024]{2,1,0:T(8,128)(2,1)} %get-tuple-element.16), channel_id=1, source_target_pairs={{96,0},{104,8},{112,16},{120,24},{0,32},{8,40},{16,48},{24,56},{32... | collective-permute-start | bytes 786440 | tf_op jit(solution)/shard_map/ppermute | solution.py:31
  65.0 0.1 maximum_maximum_fusion.refs_2_
  65.1 0.0 collective-permute-done.11.refs_6_.refs_14_
  65.1 6.8 %collective-permute-start = (bf16[528,128]{1,0:T(8,128)(2,1)S(1)}, bf16[528,128]{1,0:T(8,128)(2,1)S(1)}, u32[]{:S(2)}, u32[]{:S(2)}) collective-permute-start(bf16[528,128]{1,0:T(8,128)(2,1)S(1)} %maximum_maximum_fusion.refs_2_), channel_id=1, source_target_pairs={{0,8},{8,16},{16,24},{24,32},{32,40},{40,48},{48,56},{56,64},{64,7... | collective-permute-start | bytes 405512 | tf_op jit(solution)/shard_map/ppermute | solution.py:466
  71.9 0.0 collective-permute-done.12.refs_7_.refs_15_
  71.9 0.0 collective-permute-done.7.refs_1_.refs_9_
  71.9 0.0 copy-start.6
  72.0 11.4 %collective-permute-done.8.refs_2_.refs_10_ = bf16[2,64,1024]{2,1,0:T(8,128)(2,1)S(1)} collective-permute-done((bf16[2,64,1024]{2,1,0:T(8,128)(2,1)}, bf16[2,64,1024]{2,1,0:T(8,128)(2,1)S(1)}, u32[]{:S(2)}, u32[]{:S(2)}) %collective-permute-start.8) | collective-permute-done | bytes 262176 | tf_op jit(solution)/shard_map/ppermute | solution.py:31
  83.3 2.3 %collective-permute-done.9.refs_3_.refs_11_ = bf16[2,64,1024]{2,1,0:T(8,128)(2,1)S(1)} collective-permute-done((bf16[2,64,1024]{2,1,0:T(8,128)(2,1)}, bf16[2,64,1024]{2,1,0:T(8,128)(2,1)S(1)}, u32[]{:S(2)}, u32[]{:S(2)}) %collective-permute-start.9) | collective-permute-done | bytes 262176 | tf_op jit(solution)/shard_map/ppermute | solution.py:31
  85.7 0.7 copy-done.8
  86.3 2.9 %rank_part.1.refs_0_ = bf16[128,128]{1,0:T(8,128)(2,1)} custom-call(s32[2]{0:T(128)} %pad_add_fusion.1.meta_ref, s32[64]{0:T(128)} %slot_ref.5, s32[17]{0:T(128)} %segment_ref.5, bf16[256,1024]{1,0:T(8,128)(2,1)} %tokens_ref.1, bf16[2,64,1024]{2,1,0:T(8,128)(2,1)} %get-tuple-element.13.refs_0_.refs_8_, bf16[2,64,1024]{2,1,0:T(8,128)(2,1)} %copy-done.6, ...), custom_call_target="tpu_custom_call" | custom-call | tf_op jit(solution)/shard_map/rank_part/pallas_call | solution.py:147
  89.3 2.4 %collective-permute-start.13 = (bf16[128,128]{1,0:T(8,128)(2,1)}, bf16[128,128]{1,0:T(8,128)(2,1)S(1)}, u32[]{:S(2)}, u32[]{:S(2)}) collective-permute-start(bf16[128,128]{1,0:T(8,128)(2,1)} %rank_part.1.refs_0_), channel_id=1, source_target_pairs={{1,0},{0,1},{3,2},{2,3},{5,4},{4,5},{7,6},{6,7},{9,8},{8,9},{11,10... | collective-permute-start | bytes 98312 | tf_op jit(solution)/shard_map/ppermute | solution.py:39
  91.7 3.6 %collective-permute-start.14 = (bf16[128,128]{1,0:T(8,128)(2,1)}, bf16[128,128]{1,0:T(8,128)(2,1)S(1)}, u32[]{:S(2)}, u32[]{:S(2)}) collective-permute-start(bf16[128,128]{1,0:T(8,128)(2,1)} %rank_part.1.refs_0_), channel_id=1, source_target_pairs={{2,0},{3,1},{4,2},{5,3},{6,4},{7,5},{0,6},{1,7},{10,8},{11,9},{12,... | collective-permute-start | bytes 98312 | tf_op jit(solution)/shard_map/ppermute | solution.py:39
  95.3 0.0 collective-permute-done.refs_3_
  95.3 0.5 slice.16
  96.5 0.4 collective-permute-start.15
  96.9 0.0 collective-permute-start.16
  96.9 3.4 %collective-permute-start.17 = (bf16[128,128]{1,0:T(8,128)(2,1)}, bf16[128,128]{1,0:T(8,128)(2,1)S(1)}, u32[]{:S(2)}, u32[]{:S(2)}) collective-permute-start(bf16[128,128]{1,0:T(8,128)(2,1)} %rank_part.1.refs_0_), channel_id=1, source_target_pairs={{5,0},{4,1},{7,2},{6,3},{1,4},{0,5},{3,6},{2,7},{13,8},{12,9},{15,... | collective-permute-start | bytes 98312 | tf_op jit(solution)/shard_map/ppermute | solution.py:39
  100.2 0.0 collective-permute-done.13.refs_1_
  100.2 1.3 collective-permute-start.18
  101.6 0.0 collective-permute-done.14.refs_2_
  101.6 0.0 collective-permute-start.19
  101.6 1.8 %pad_add_fusion.refs_0_ = s32[3]{0:T(128)} fusion(s32[1]{0:T(128)} %bitcast.3, s32[1]{0:T(128)} %bitcast.1, s32[1]{0:T(128)} %slice.12), kind=kLoop, calls=%fused_computation.4 | loop fusion | flops 6 | bytes 24 | tf_op jit(solution)/shard_map/concatenate | solution.py:472
  103.4 0.0 collective-permute-done.15.refs_3_
  103.4 0.0 collective-permute-done.16.refs_4_
  103.4 0.0 collective-permute-done.17.refs_5_
  103.5 0.9 collective-permute-done.18.refs_6_
  104.4 1.9 %collective-permute-done.19.refs_7_ = bf16[128,128]{1,0:T(8,128)(2,1)S(1)} collective-permute-done((bf16[128,128]{1,0:T(8,128)(2,1)}, bf16[128,128]{1,0:T(8,128)(2,1)S(1)}, u32[]{:S(2)}, u32[]{:S(2)}) %collective-permute-start.19) | collective-permute-done | bytes 32800 | tf_op jit(solution)/shard_map/ppermute | solution.py:39
  106.4 0.6 copy-done.24
  107.0 3.3 %queries.1.refs_1_ = bf16[2560,128]{1,0:T(8,128)(2,1)} custom-call(s32[2]{0:T(128)} %pad_add_fusion.1.meta_ref, s32[64]{0:T(128)} %slot_ref.5, s32[17]{0:T(128)} %segment_ref.5, bf16[256,1024]{1,0:T(8,128)(2,1)} %base_ref.1, bf16[128,128]{1,0:T(8,128)(2,1)} %rank_part.1.refs_0_, bf16[128,128]{1,0:T(8,128)(2,1)} %copy-done.18, bf16[128,128]{1,0:T(8,128)(2,1)} %copy-done.19, ...), custom_call_target="tpu_custom_call" | custom-call | tf_op jit(solution)/shard_map/queries/pallas_call | solution.py:202
  110.3 0.0 all-gather.2.cloned.1.call-done.refs_4_
  110.4 36.7 %attend.1 = bf16[256,1024]{1,0:T(8,128)(2,1)} custom-call(s32[3]{0:T(128)} %pad_add_fusion.refs_0_, bf16[2560,128]{1,0:T(8,128)(2,1)} %queries.1.refs_1_, bf16[528,128]{1,0:T(8,128)(2,1)} %copy-done.9, bf16[528,128]{1,0:T(8,128)(2,1)} %copy-done.15, bf16[33024,128]{1,0:T(8,128)(2,1)} %all-gather.2.cloned.1.call-done.refs_4_), custom_call_target="tpu_custom_call" | custom-call | tf_op jit(solution)/shard_map/attend/pallas_call | solution.py:403
  (48 shorter events, 0.1 us)
Async XLA Ops:
  6.5 2.7 %copy-start.2 = (bf16[4,2,64,1024]{3,2,1,0:T(8,128)(2,1)S(1)}, bf16[4,2,64,1024]{3,2,1,0:T(8,128)(2,1)}, u32[]{:S(2)}) copy-start(bf16[4,2,64,1024]{3,2,1,0:T(8,128)(2,1)} %param.17) | copy-start | bytes 3145732
  6.5 103.8 %all-gather.2.cloned.1.call-start = ((), (), s32[]{:S(2)}) async-start(), calls=%async_computation | async-start | bytes 8982528 | tf_op jit(solution)/shard_map/all_gather | solution.py:453
  9.2 15.5 %copy-start.25 = (s32[256]{0:T(256)S(1)}, s32[256]{0:T(256)}, u32[]{:S(2)}) copy-start(s32[256]{0:T(256)} %param.20) | copy-start | bytes 3076
  9.3 38.6 %copy-start = (bf16[4,2,32,1024]{3,2,1,0:T(8,128)(2,1)}, bf16[4,2,32,1024]{3,2,1,0:T(8,128)(2,1)S(1)}, u32[]{:S(2)}) copy-start(bf16[4,2,32,1024]{3,2,1,0:T(8,128)(2,1)S(1)} %get-tuple-element.21) | copy-start | bytes 1572868
  9.3 38.6 %copy-start.1 = (bf16[4,2,32,1024]{3,2,1,0:T(8,128)(2,1)}, bf16[4,2,32,1024]{3,2,1,0:T(8,128)(2,1)S(1)}, u32[]{:S(2)}) copy-start(bf16[4,2,32,1024]{3,2,1,0:T(8,128)(2,1)S(1)} %get-tuple-element.22) | copy-start | bytes 1572868
  9.3 13.9 %collective-permute-start.1 = (bf16[4,64,1024]{2,1,0:T(8,128)(2,1)S(1)}, bf16[4,64,1024]{2,1,0:T(8,128)(2,1)S(1)}, u32[]{:S(2)}, u32[]{:S(2)}) collective-permute-start(bf16[4,64,1024]{2,1,0:T(8,128)(2,1)S(1)} %bitcast.11), channel_id=1, source_target_pairs={{8,0},{16,8},{24,16},{0,24},{40,32},{48,40},{56,48},{32,56},{72,64... | collective-permute-start | bytes 1572872 | tf_op jit(solution)/shard_map/ppermute | solution.py:31
  11.9 16.5 %collective-permute-start.2 = (bf16[4,64,1024]{2,1,0:T(8,128)(2,1)S(1)}, bf16[4,64,1024]{2,1,0:T(8,128)(2,1)S(1)}, u32[]{:S(2)}, u32[]{:S(2)}) collective-permute-start(bf16[4,64,1024]{2,1,0:T(8,128)(2,1)S(1)} %bitcast.12), channel_id=1, source_target_pairs={{16,0},{24,8},{0,16},{8,24},{48,32},{56,40},{32,48},{40,56},{80,64... | collective-permute-start | bytes 1572872 | tf_op jit(solution)/shard_map/ppermute | solution.py:31
  12.4 34.7 %collective-permute-start.3 = (bf16[4,64,1024]{2,1,0:T(8,128)(2,1)S(1)}, bf16[4,64,1024]{2,1,0:T(8,128)(2,1)S(1)}, u32[]{:S(2)}, u32[]{:S(2)}) collective-permute-start(bf16[4,64,1024]{2,1,0:T(8,128)(2,1)S(1)} %bitcast.13), channel_id=1, source_target_pairs={{24,0},{0,8},{8,16},{16,24},{56,32},{32,40},{40,48},{48,56},{88,64... | collective-permute-start | bytes 1572872 | tf_op jit(solution)/shard_map/ppermute | solution.py:31
  13.0 34.1 %collective-permute-start.4 = (bf16[4,64,1024]{2,1,0:T(8,128)(2,1)S(1)}, bf16[4,64,1024]{2,1,0:T(8,128)(2,1)S(1)}, u32[]{:S(2)}, u32[]{:S(2)}) collective-permute-start(bf16[4,64,1024]{2,1,0:T(8,128)(2,1)S(1)} %bitcast.7), channel_id=1, source_target_pairs={{32,0},{40,8},{48,16},{56,24},{64,32},{72,40},{80,48},{88,56},{96,... | collective-permute-start | bytes 1572872 | tf_op jit(solution)/shard_map/ppermute | solution.py:31
  13.5 33.6 %collective-permute-start.5 = (bf16[4,64,1024]{2,1,0:T(8,128)(2,1)S(1)}, bf16[4,64,1024]{2,1,0:T(8,128)(2,1)S(1)}, u32[]{:S(2)}, u32[]{:S(2)}) collective-permute-start(bf16[4,64,1024]{2,1,0:T(8,128)(2,1)S(1)} %bitcast.8), channel_id=1, source_target_pairs={{64,0},{72,8},{80,16},{88,24},{96,32},{104,40},{112,48},{120,56},{... | collective-permute-start | bytes 1572872 | tf_op jit(solution)/shard_map/ppermute | solution.py:31
  23.3 24.7 %copy-start.10 = (bf16[4,64,1024]{2,1,0:T(8,128)(2,1)}, bf16[4,64,1024]{2,1,0:T(8,128)(2,1)S(1)}, u32[]{:S(2)}) copy-start(bf16[4,64,1024]{2,1,0:T(8,128)(2,1)S(1)} %collective-permute-done.1.refs_1_) | copy-start | bytes 1572868
  23.3 24.7 %collective-permute-start.6 = (bf16[4,64,1024]{2,1,0:T(8,128)(2,1)S(1)}, bf16[4,64,1024]{2,1,0:T(8,128)(2,1)}, u32[]{:S(2)}, u32[]{:S(2)}) collective-permute-start(bf16[4,64,1024]{2,1,0:T(8,128)(2,1)S(1)} %bitcast.9), channel_id=1, source_target_pairs={{96,0},{104,8},{112,16},{120,24},{0,32},{8,40},{16,48},{24,56},{32... | collective-permute-start | bytes 1572872 | tf_op jit(solution)/shard_map/ppermute | solution.py:31
  28.3 36.6 %copy-start.16 = (bf16[256,128]{1,0:T(8,128)(2,1)S(1)}, bf16[256,128]{1,0:T(8,128)(2,1)}, u32[]{:S(2)}) copy-start(bf16[256,128]{1,0:T(8,128)(2,1)} %param.14) | copy-start | bytes 196612
  28.3 36.6 %copy-start.17 = (bf16[256,128]{1,0:T(8,128)(2,1)S(1)}, bf16[256,128]{1,0:T(8,128)(2,1)}, u32[]{:S(2)}) copy-start(bf16[256,128]{1,0:T(8,128)(2,1)} %param.13) | copy-start | bytes 196612
  28.3 19.6 %copy-start.11 = (bf16[4,64,1024]{2,1,0:T(8,128)(2,1)}, bf16[4,64,1024]{2,1,0:T(8,128)(2,1)S(1)}, u32[]{:S(2)}) copy-start(bf16[4,64,1024]{2,1,0:T(8,128)(2,1)S(1)} %collective-permute-done.2.refs_2_) | copy-start | bytes 1572868
  47.1 1.0 copy-start.12
  47.1 1.2 copy-start.13
  47.1 0.9 copy-start.14
  52.1 7.9 %collective-permute-start.10 = (bf16[2,64,1024]{2,1,0:T(8,128)(2,1)}, bf16[2,64,1024]{2,1,0:T(8,128)(2,1)S(1)}, u32[]{:S(2)}, u32[]{:S(2)}) collective-permute-start(bf16[2,64,1024]{2,1,0:T(8,128)(2,1)} %get-tuple-element.18), channel_id=1, source_target_pairs={{8,0},{16,8},{24,16},{0,24},{40,32},{48,40},{56,48},{32,56},{72,64... | collective-permute-start | bytes 786440 | tf_op jit(solution)/shard_map/ppermute | solution.py:31
  52.4 12.7 %collective-permute-start.11 = (bf16[2,64,1024]{2,1,0:T(8,128)(2,1)}, bf16[2,64,1024]{2,1,0:T(8,128)(2,1)S(1)}, u32[]{:S(2)}, u32[]{:S(2)}) collective-permute-start(bf16[2,64,1024]{2,1,0:T(8,128)(2,1)} %get-tuple-element.19), channel_id=1, source_target_pairs={{16,0},{24,8},{0,16},{8,24},{48,32},{56,40},{32,48},{40,56},{80,64... | collective-permute-start | bytes 786440 | tf_op jit(solution)/shard_map/ppermute | solution.py:31
  55.1 16.8 %collective-permute-start.12 = (bf16[2,64,1024]{2,1,0:T(8,128)(2,1)}, bf16[2,64,1024]{2,1,0:T(8,128)(2,1)S(1)}, u32[]{:S(2)}, u32[]{:S(2)}) collective-permute-start(bf16[2,64,1024]{2,1,0:T(8,128)(2,1)} %get-tuple-element.20), channel_id=1, source_target_pairs={{24,0},{0,8},{8,16},{16,24},{56,32},{32,40},{40,48},{48,56},{88,64... | collective-permute-start | bytes 786440 | tf_op jit(solution)/shard_map/ppermute | solution.py:31
  55.2 16.7 %collective-permute-start.7 = (bf16[2,64,1024]{2,1,0:T(8,128)(2,1)}, bf16[2,64,1024]{2,1,0:T(8,128)(2,1)S(1)}, u32[]{:S(2)}, u32[]{:S(2)}) collective-permute-start(bf16[2,64,1024]{2,1,0:T(8,128)(2,1)} %get-tuple-element.14), channel_id=1, source_target_pairs={{32,0},{40,8},{48,16},{56,24},{64,32},{72,40},{80,48},{88,56},{96,... | collective-permute-start | bytes 786440 | tf_op jit(solution)/shard_map/ppermute | solution.py:31
  56.7 26.6 %collective-permute-start.8 = (bf16[2,64,1024]{2,1,0:T(8,128)(2,1)}, bf16[2,64,1024]{2,1,0:T(8,128)(2,1)S(1)}, u32[]{:S(2)}, u32[]{:S(2)}) collective-permute-start(bf16[2,64,1024]{2,1,0:T(8,128)(2,1)} %get-tuple-element.15), channel_id=1, source_target_pairs={{64,0},{72,8},{80,16},{88,24},{96,32},{104,40},{112,48},{120,56},{... | collective-permute-start | bytes 786440 | tf_op jit(solution)/shard_map/ppermute | solution.py:31
  60.0 25.7 %copy-start.3 = (bf16[2,64,1024]{2,1,0:T(8,128)(2,1)}, bf16[2,64,1024]{2,1,0:T(8,128)(2,1)S(1)}, u32[]{:S(2)}) copy-start(bf16[2,64,1024]{2,1,0:T(8,128)(2,1)S(1)} %collective-permute-done.10.refs_5_.refs_13_) | copy-start | bytes 786436
  60.0 25.7 %collective-permute-start.9 = (bf16[2,64,1024]{2,1,0:T(8,128)(2,1)}, bf16[2,64,1024]{2,1,0:T(8,128)(2,1)S(1)}, u32[]{:S(2)}, u32[]{:S(2)}) collective-permute-start(bf16[2,64,1024]{2,1,0:T(8,128)(2,1)} %get-tuple-element.16), channel_id=1, source_target_pairs={{96,0},{104,8},{112,16},{120,24},{0,32},{8,40},{16,48},{24,56},{32... | collective-permute-start | bytes 786440 | tf_op jit(solution)/shard_map/ppermute | solution.py:31
  65.1 45.2 %copy-start.9 = (bf16[528,128]{1,0:T(8,128)(2,1)}, bf16[528,128]{1,0:T(8,128)(2,1)S(1)}, u32[]{:S(2)}) copy-start(bf16[528,128]{1,0:T(8,128)(2,1)S(1)} %maximum_maximum_fusion.refs_2_) | copy-start | bytes 405508
  65.1 20.5 %copy-start.4 = (bf16[2,64,1024]{2,1,0:T(8,128)(2,1)}, bf16[2,64,1024]{2,1,0:T(8,128)(2,1)S(1)}, u32[]{:S(2)}) copy-start(bf16[2,64,1024]{2,1,0:T(8,128)(2,1)S(1)} %collective-permute-done.11.refs_6_.refs_14_) | copy-start | bytes 786436
  65.1 30.2 %collective-permute-start = (bf16[528,128]{1,0:T(8,128)(2,1)S(1)}, bf16[528,128]{1,0:T(8,128)(2,1)S(1)}, u32[]{:S(2)}, u32[]{:S(2)}) collective-permute-start(bf16[528,128]{1,0:T(8,128)(2,1)S(1)} %maximum_maximum_fusion.refs_2_), channel_id=1, source_target_pairs={{0,8},{8,16},{16,24},{24,32},{32,40},{40,48},{48,56},{56,64},{64,7... | collective-permute-start | bytes 405512 | tf_op jit(solution)/shard_map/ppermute | solution.py:466
  71.9 13.7 %copy-start.5 = (bf16[2,64,1024]{2,1,0:T(8,128)(2,1)}, bf16[2,64,1024]{2,1,0:T(8,128)(2,1)S(1)}, u32[]{:S(2)}) copy-start(bf16[2,64,1024]{2,1,0:T(8,128)(2,1)S(1)} %collective-permute-done.12.refs_7_.refs_15_) | copy-start | bytes 786436
  71.9 13.7 %copy-start.6 = (bf16[2,64,1024]{2,1,0:T(8,128)(2,1)}, bf16[2,64,1024]{2,1,0:T(8,128)(2,1)S(1)}, u32[]{:S(2)}) copy-start(bf16[2,64,1024]{2,1,0:T(8,128)(2,1)S(1)} %collective-permute-done.7.refs_1_.refs_9_) | copy-start | bytes 786436
  83.3 2.4 %copy-start.7 = (bf16[2,64,1024]{2,1,0:T(8,128)(2,1)}, bf16[2,64,1024]{2,1,0:T(8,128)(2,1)S(1)}, u32[]{:S(2)}) copy-start(bf16[2,64,1024]{2,1,0:T(8,128)(2,1)S(1)} %collective-permute-done.8.refs_2_.refs_10_) | copy-start | bytes 786436
  85.6 0.7 copy-start.8
  89.3 11.0 %collective-permute-start.13 = (bf16[128,128]{1,0:T(8,128)(2,1)}, bf16[128,128]{1,0:T(8,128)(2,1)S(1)}, u32[]{:S(2)}, u32[]{:S(2)}) collective-permute-start(bf16[128,128]{1,0:T(8,128)(2,1)} %rank_part.1.refs_0_), channel_id=1, source_target_pairs={{1,0},{0,1},{3,2},{2,3},{5,4},{4,5},{7,6},{6,7},{9,8},{8,9},{11,10... | collective-permute-start | bytes 98312 | tf_op jit(solution)/shard_map/ppermute | solution.py:39
  91.7 9.9 %collective-permute-start.14 = (bf16[128,128]{1,0:T(8,128)(2,1)}, bf16[128,128]{1,0:T(8,128)(2,1)S(1)}, u32[]{:S(2)}, u32[]{:S(2)}) collective-permute-start(bf16[128,128]{1,0:T(8,128)(2,1)} %rank_part.1.refs_0_), channel_id=1, source_target_pairs={{2,0},{3,1},{4,2},{5,3},{6,4},{7,5},{0,6},{1,7},{10,8},{11,9},{12,... | collective-permute-start | bytes 98312 | tf_op jit(solution)/shard_map/ppermute | solution.py:39
  95.3 15.0 %copy-start.15 = (bf16[528,128]{1,0:T(8,128)(2,1)}, bf16[528,128]{1,0:T(8,128)(2,1)S(1)}, u32[]{:S(2)}) copy-start(bf16[528,128]{1,0:T(8,128)(2,1)S(1)} %collective-permute-done.refs_3_) | copy-start | bytes 405508
  96.5 7.0 %collective-permute-start.15 = (bf16[128,128]{1,0:T(8,128)(2,1)}, bf16[128,128]{1,0:T(8,128)(2,1)S(1)}, u32[]{:S(2)}, u32[]{:S(2)}) collective-permute-start(bf16[128,128]{1,0:T(8,128)(2,1)} %rank_part.1.refs_0_), channel_id=1, source_target_pairs={{3,0},{2,1},{5,2},{4,3},{7,4},{6,5},{1,6},{0,7},{11,8},{10,9},{13,... | collective-permute-start | bytes 98312 | tf_op jit(solution)/shard_map/ppermute | solution.py:39
  96.9 6.6 %collective-permute-start.16 = (bf16[128,128]{1,0:T(8,128)(2,1)}, bf16[128,128]{1,0:T(8,128)(2,1)S(1)}, u32[]{:S(2)}, u32[]{:S(2)}) collective-permute-start(bf16[128,128]{1,0:T(8,128)(2,1)} %rank_part.1.refs_0_), channel_id=1, source_target_pairs={{4,0},{5,1},{6,2},{7,3},{0,4},{1,5},{2,6},{3,7},{12,8},{13,9},{14,... | collective-permute-start | bytes 98312 | tf_op jit(solution)/shard_map/ppermute | solution.py:39
  96.9 6.6 %collective-permute-start.17 = (bf16[128,128]{1,0:T(8,128)(2,1)}, bf16[128,128]{1,0:T(8,128)(2,1)S(1)}, u32[]{:S(2)}, u32[]{:S(2)}) collective-permute-start(bf16[128,128]{1,0:T(8,128)(2,1)} %rank_part.1.refs_0_), channel_id=1, source_target_pairs={{5,0},{4,1},{7,2},{6,3},{1,4},{0,5},{3,6},{2,7},{13,8},{12,9},{15,... | collective-permute-start | bytes 98312 | tf_op jit(solution)/shard_map/ppermute | solution.py:39
  100.2 6.1 %copy-start.18 = (bf16[128,128]{1,0:T(8,128)(2,1)}, bf16[128,128]{1,0:T(8,128)(2,1)S(1)}, u32[]{:S(2)}) copy-start(bf16[128,128]{1,0:T(8,128)(2,1)S(1)} %collective-permute-done.13.refs_1_) | copy-start | bytes 98308
  100.2 4.2 %collective-permute-start.18 = (bf16[128,128]{1,0:T(8,128)(2,1)}, bf16[128,128]{1,0:T(8,128)(2,1)S(1)}, u32[]{:S(2)}, u32[]{:S(2)}) collective-permute-start(bf16[128,128]{1,0:T(8,128)(2,1)} %rank_part.1.refs_0_), channel_id=1, source_target_pairs={{6,0},{7,1},{0,2},{1,3},{2,4},{3,5},{4,6},{5,7},{14,8},{15,9},{8,1... | collective-permute-start | bytes 98312 | tf_op jit(solution)/shard_map/ppermute | solution.py:39
  101.6 4.8 %copy-start.19 = (bf16[128,128]{1,0:T(8,128)(2,1)}, bf16[128,128]{1,0:T(8,128)(2,1)S(1)}, u32[]{:S(2)}) copy-start(bf16[128,128]{1,0:T(8,128)(2,1)S(1)} %collective-permute-done.14.refs_2_) | copy-start | bytes 98308
  101.6 4.8 %collective-permute-start.19 = (bf16[128,128]{1,0:T(8,128)(2,1)}, bf16[128,128]{1,0:T(8,128)(2,1)S(1)}, u32[]{:S(2)}, u32[]{:S(2)}) collective-permute-start(bf16[128,128]{1,0:T(8,128)(2,1)} %rank_part.1.refs_0_), channel_id=1, source_target_pairs={{7,0},{6,1},{1,2},{0,3},{3,4},{2,5},{5,6},{4,7},{15,8},{14,9},{9,1... | collective-permute-start | bytes 98312 | tf_op jit(solution)/shard_map/ppermute | solution.py:39
  103.4 2.9 %copy-start.20 = (bf16[128,128]{1,0:T(8,128)(2,1)}, bf16[128,128]{1,0:T(8,128)(2,1)S(1)}, u32[]{:S(2)}) copy-start(bf16[128,128]{1,0:T(8,128)(2,1)S(1)} %collective-permute-done.15.refs_3_) | copy-start | bytes 98308
  103.4 2.9 %copy-start.21 = (bf16[128,128]{1,0:T(8,128)(2,1)}, bf16[128,128]{1,0:T(8,128)(2,1)S(1)}, u32[]{:S(2)}) copy-start(bf16[128,128]{1,0:T(8,128)(2,1)S(1)} %collective-permute-done.16.refs_4_) | copy-start | bytes 98308
  103.5 2.9 %copy-start.22 = (bf16[128,128]{1,0:T(8,128)(2,1)}, bf16[128,128]{1,0:T(8,128)(2,1)S(1)}, u32[]{:S(2)}) copy-start(bf16[128,128]{1,0:T(8,128)(2,1)S(1)} %collective-permute-done.17.refs_5_) | copy-start | bytes 98308
  104.4 2.0 %copy-start.23 = (bf16[128,128]{1,0:T(8,128)(2,1)}, bf16[128,128]{1,0:T(8,128)(2,1)S(1)}, u32[]{:S(2)}) copy-start(bf16[128,128]{1,0:T(8,128)(2,1)S(1)} %collective-permute-done.18.refs_6_) | copy-start | bytes 98308
  106.4 0.6 copy-start.24
Sparse Core Ops, SparseCore 0:
  9.6 97.5 all-gather.1

commit v3 on v2

--- a/solution.py
+++ b/solution.py
@@ -49,7 +49,7 @@
 
 
 def pick_kernel(meta_ref, slot_ref, segment_ref, *refs):
-    bufs, outs, sems = refs[0:8], refs[8:16], refs[16]
+    bufs, outs, sems = refs[0:10], refs[10:18], refs[18]
     me = meta_ref[0]
     for f, along_x in enumerate((True, False)):
         along, across = place(me, along_x)
@@ -60,11 +60,19 @@
                 row = stored_row(slot_ref, segment_ref, dest + k)
                 owner_along, _ = place(row // 4, along_x)
                 ring = lax.rem(owner_along - along + SIDE, SIDE)
-                for b in range(SIDE):
-                    @pl.when(ring == b)
+                index = lax.rem(row, 4)
+                cases = (
+                    (ring == 0, index),
+                    (ring == 1, index),
+                    (ring == 3, index),
+                    ((ring == 2) & (index < 2), index),
+                    ((ring == 2) & (index >= 2), index - 2),
+                )
+                for b, (found, at) in enumerate(cases):
+                    @pl.when(found)
                     def _():
                         pltpu.make_async_copy(
-                            bufs[f * 4 + b].at[lax.rem(row, 4)],
+                            bufs[f * 5 + b].at[at],
                             outs[f * 4 + d].at[k],
                             sems.at[f * 8 + d * 2 + k],
                         ).start()
@@ -72,7 +80,7 @@
         for d in range(SIDE):
             for k in range(2):
                 pltpu.make_async_copy(
-                    bufs[f * 4].at[0], outs[f * 4 + d].at[k], sems.at[f * 8 + d * 2 + k]
+                    bufs[f * 5].at[0], outs[f * 4 + d].at[k], sems.at[f * 8 + d * 2 + k]
                 ).wait()
 
 
@@ -82,7 +90,7 @@
     return pl.pallas_call(
         pick_kernel,
         out_shape=[out] * 8,
-        in_specs=[smem] * 3 + [pl.BlockSpec(memory_space=pl.ANY)] * 8,
+        in_specs=[smem] * 3 + [pl.BlockSpec(memory_space=pl.ANY)] * 10,
         out_specs=[pl.BlockSpec(memory_space=pltpu.VMEM)] * 8,
         scratch_shapes=[pltpu.SemaphoreType.DMA((16,))],
         name="pick_items",
@@ -90,9 +98,12 @@
 
 
 def ring_rows(raw_x, raw_y):
+    after_x, before_x = pull(raw_x, 1, 0), pull(raw_x, -1, 0)
+    after_y, before_y = pull(raw_y, 0, 1), pull(raw_y, 0, -1)
+    half = raw_x.shape[0] // 2
     return [
-        raw_x, pull(raw_x, 1, 0), pull(raw_x, 2, 0), pull(raw_x, -1, 0),
-        raw_y, pull(raw_y, 0, 1), pull(raw_y, 0, 2), pull(raw_y, 0, -1),
+        raw_x, after_x, before_x, pull(after_x[:half], 1, 0), pull(before_x[half:], -1, 0),
+        raw_y, after_y, before_y, pull(after_y[:half], 0, 1), pull(before_y[half:], 0, -1),
     ]
 
 
@@ -155,7 +166,7 @@
 
 
 def query_kernel(meta_ref, slot_ref, segment_ref, base_ref, *refs):
-    parts, got, q_ref, up = refs[0:8], refs[8:16], refs[16], refs[17]
+    parts, got, q_ref, up = refs[0:4], refs[4:12], refs[12], refs[13]
 
     def store(k, offset, block):
         for start in ((k * RANK), (3 - k) * RANK):
@@ -202,7 +213,7 @@
     return pl.pallas_call(
         query_kernel,
         out_shape=jax.ShapeDtypeStruct((rows * HEADS + STEP_ROWS, HEAD_SIZE), jnp.bfloat16),
-        in_specs=[smem] * 3 + [vmem] * 17,
+        in_specs=[smem] * 3 + [vmem] * 13,
         out_specs=vmem,
         scratch_shapes=[pltpu.VMEM((4 * RANK, width), jnp.bfloat16)],
         compiler_params=pltpu.CompilerParams(vmem_limit_bytes=VMEM_LIMIT),
@@ -220,7 +231,7 @@
     groups = k_sc.shape[0] // 2 // keys_step
     own_rows = cache_ref.shape[0] // blocks
     own_pages = (own_rows - 16) // (2 * PAGE)
-    seg_a, cut, prev_cut = meta_ref[0], meta_ref[1], meta_ref[2]
+    seg_a, cut = meta_ref[0], meta_ref[1]
 
     for d in range(blocks):
         pltpu.make_async_copy(
@@ -257,41 +268,6 @@
         al_sc[rows, 0:128] = al_sc[rows, 0:128] * fade + added[:, 0:128]
         al_sc[rows, 128:256] = al_sc[rows, 128:256] * fade + added[:, 128:256]
 
-    for d in range(blocks):
-        pltpu.make_async_copy(
-            cache_ref.at[pl.ds((d + 1) * own_rows - 16, 16)], id_rows.at[d], id_sem.at[d]
-        ).wait()
-    for d in range(blocks):
-        id_vec[d:d + 1, :] = id_rows[d].astype(jnp.int32)[0:1, :]
-    copy = pltpu.make_async_copy(id_vec, id_sc, id_sem.at[0])
-    copy.start()
-    copy.wait()
-
-    count_sc[0] = 0
-    count_sc[1] = 0
-
-    def page_copies(d, page, slot):
-        here = pl.ds(pl.multiple_of(slot * PAGE, PAGE), PAGE)
-        at = pl.multiple_of(d * own_rows + page * PAGE, 16)
-        keys = pltpu.make_async_copy(cache_ref.at[pl.ds(at, PAGE)], k_sc.at[here], k_sem)
-        at = pl.multiple_of(d * own_rows + (own_pages + page) * PAGE, 16)
-        values = pltpu.make_async_copy(
-            cache_ref.at[pl.ds(at, PAGE)], v_sc.at[here, pl.ds(0, 128)], v_sem
-        )
-        return keys, values
-
-    @pl.loop(0, blocks * own_pages)
-    def _(i):
-        d, page = i // own_pages, lax.rem(i, own_pages)
-        which = id_sc[d, page] - seg_a
-
-        @pl.when((which == 0) | (which == 1))
-        def _():
-            n = count_sc[which]
-            for c in page_copies(d, page, which * groups * GROUP + n):
-                c.start()
-            count_sc[which] = n + 1
-
     span_keys = jnp.concatenate([prev_ref[0:256, :], span_ref[0:256, :]], axis=0)
     span_values = jnp.concatenate(
         [
@@ -301,8 +277,10 @@
         axis=1,
     )
 
-    @pl.loop(0, tiles)
-    def _(t):
+    before = jnp.max(prev_ref[512:528, :].astype(jnp.float32)).astype(jnp.int32)
+    prev_cut = jnp.where(seg_a == 0, 256, before)
+
+    def span_tile(t):
         rows = rows_at(t * STEP_ROWS)
         scores = lax.dot_general(
             q_ref[rows, :], span_keys, (((1,), (1,)), ((), ())), preferred_element_type=jnp.float32
@@ -318,6 +296,46 @@
         weights = jnp.exp2(scores - peak).astype(jnp.bfloat16)
         m_sc[rows, :] = jnp.broadcast_to(peak, (STEP_ROWS, 128))
         al_sc[rows, :] = jnp.dot(weights, span_values, preferred_element_type=jnp.float32)
+
+    span_tile(0)
+    for d in range(blocks):
+        pltpu.make_async_copy(
+            cache_ref.at[pl.ds((d + 1) * own_rows - 16, 16)], id_rows.at[d], id_sem.at[d]
+        ).wait()
+    for d in range(blocks):
+        id_vec[d:d + 1, :] = id_rows[d].astype(jnp.int32)[0:1, :]
+    copy = pltpu.make_async_copy(id_vec, id_sc, id_sem.at[0])
+    copy.start()
+    span_tile(1)
+    copy.wait()
+
+    count_sc[0] = 0
+    count_sc[1] = 0
+
+    def page_copies(d, page, slot):
+        here = pl.ds(pl.multiple_of(slot * PAGE, PAGE), PAGE)
+        at = pl.multiple_of(d * own_rows + page * PAGE, 16)
+        keys = pltpu.make_async_copy(cache_ref.at[pl.ds(at, PAGE)], k_sc.at[here], k_sem)
+        at = pl.multiple_of(d * own_rows + (own_pages + page) * PAGE, 16)
+        values = pltpu.make_async_copy(
+            cache_ref.at[pl.ds(at, PAGE)], v_sc.at[here, pl.ds(0, 128)], v_sem
+        )
+        return keys, values
+
+    @pl.loop(0, blocks * own_pages)
+    def _(i):
+        d, page = i // own_pages, lax.rem(i, own_pages)
+        which = id_sc[d, page] - seg_a
+
+        @pl.when((which == 0) | (which == 1))
+        def _():
+            n = count_sc[which]
+            for c in page_copies(d, page, which * groups * GROUP + n):
+                c.start()
+            count_sc[which] = n + 1
+
+    for t in range(2, tiles):
+        span_tile(t)
 
     mixed_start = jnp.minimum(cut // TILE, tiles - 1) * STEP_ROWS
     mixed = rows_at(mixed_start)
@@ -439,8 +457,6 @@
     token_request,
     cache_doc,
 ):
-    tok_rows = tokens_in.shape[0]
-    me = lax.axis_index("ctx")
     seg_a = token_request[0]
     cut = jnp.sum((token_request == seg_a).astype(jnp.int32))
     meta = jnp.stack([seg_a, cut])
@@ -463,14 +479,14 @@
     span = jnp.concatenate(
         [fresh_keys, fresh_values, jnp.broadcast_to(cut.astype(jnp.bfloat16), (16, 128))], axis=0
     )
+    acts = rank_part(*ids, tokens_in, got)
+    pair = pull_tp(acts, 0, 1)
+    pair, span = lax.optimization_barrier((pair, span))
     prev = lax.ppermute(span, "ctx", [(i - 1, i) for i in range(1, SIDE * SIDE)])
-    prev_cut = jnp.where(me == 0, tok_rows, prev[512, 0].astype(jnp.int32))
-
-    acts = rank_part(*ids, tokens_in, got)
-    parts = [acts] + [pull_tp(acts, dz, dc) for dz in range(SIDE) for dc in range(2) if dz or dc]
+    acts = (acts.astype(jnp.float32) + pair.astype(jnp.float32)).astype(jnp.bfloat16)
+    parts = [acts] + [pull_tp(acts, dz, 0) for dz in (1, 2, 3)]
     query = queries(*ids, base_queries, parts, got)
-    info = jnp.concatenate([meta, prev_cut[None]])
-    return attend(info, query, span, prev, cache, SIDE * SIDE)
+    return attend(meta, query, span, prev, cache, SIDE * SIDE)
 
 
 def solution(mesh):

time: 154 us -> 142 us (0.922)
  the two profiles are of different devices: /device:TPU:25 before, /device:TPU:6 now
where the time goes in v3:
time: 142 us; the launch traced here: 143 us
  Pallas kernels  45.5 us (32%)
  waiting for transfers between devices  43.7 us (31%)
  starting transfers between devices  29.8 us (21%)
  between operations  14.4 us (10%)
  other arithmetic  6.72 us (5%)
  local copies, waits for them, and re-layouts  3.33 us (2%)
    ppermute x14, waiting for transfers between devices, pull(): return lax.ppermute(block, 'ctx', route)  37.9 us
    pallas_call x1, Pallas kernels, attend(): pl.pallas_call(functools.partial(attend_kernel, blocks), out_shape=jax.Sh...  35.4 us
    ppermute x14, starting transfers between devices, pull(): return lax.ppermute(block, 'ctx', route)  20.1 us
    ppermute x4, waiting for transfers between devices, pull_tp(): return lax.ppermute(block, 'tp', route)  5.72 us
    ppermute x4, starting transfers between devices, pull_tp(): return lax.ppermute(block, 'tp', route)  5.54 us
    ppermute x1, starting transfers between devices, per_device(): lax.ppermute(span, 'ctx', [(i - 1, i) for i in range(1, SIDE * SIDE)])  4.22 us
    pallas_call x1, Pallas kernels, pick(): pl.pallas_call(pick_kernel, out_shape=[out] * 8, in_specs=[smem] * 3 + [p...  3.82 us
    pallas_call x1, Pallas kernels, queries(): pl.pallas_call(query_kernel, out_shape=jax.ShapeDtypeStruct((rows * HEADS...  3.27 us
  transfers between devices with their start and end apart: 20, of which 13 were waited for; matrix products, arithmetic and copies ran while one was open for 3% of the time, Pallas kernels for 7%

profile of v3, /device:TPU:6, one launch (start us, length us, event | category | flops | bytes accessed | tf_op | source)
XLA Modules:
  0.0 143.4 jit_solution(11836588134679127760)
XLA Ops:
  6.5 0.7 convert.4
  7.3 1.9 %pad_maximum_fusion = bf16[2064,128]{1,0:T(8,128)(2,1)} fusion(bf16[16,128]{1,0:T(8,128)(2,1)S(1)} %broadcast_in_dim.10, bf16[1024,128]{1,0:T(8,128)(2,1)} %param.16, bf16[1024,128]{1,0:T(8,128)(2,1)} %param.15), kind=kLoop, calls=%fused_computation | loop fusion | flops 1585152 | bytes 1056768 | tf_op jit(solution)/shard_map/concatenate | solution.py:466
  9.2 0.0 all-gather.2.cloned.1.call-update
  9.2 0.1 fusion.1
  9.3 0.0 copy-start
  9.3 0.0 copy-start.1
  9.3 0.0 copy-start.22
  9.4 0.9 collective-permute-start
  10.2 2.4 %collective-permute-start.1 = (bf16[4,64,1024]{2,1,0:T(8,128)(2,1)S(1)}, bf16[4,64,1024]{2,1,0:T(8,128)(2,1)S(1)}, u32[]{:S(2)}, u32[]{:S(2)}) collective-permute-start(bf16[4,64,1024]{2,1,0:T(8,128)(2,1)S(1)} %bitcast.8), channel_id=1, source_target_pairs={{24,0},{0,8},{8,16},{16,24},{56,32},{32,40},{40,48},{48,56},{88,64... | collective-permute-start | bytes 1572872 | tf_op jit(solution)/shard_map/ppermute | solution.py:31
  12.7 3.0 %collective-permute-start.4 = (bf16[4,64,1024]{2,1,0:T(8,128)(2,1)S(1)}, bf16[4,64,1024]{2,1,0:T(8,128)(2,1)S(1)}, u32[]{:S(2)}, u32[]{:S(2)}) collective-permute-start(bf16[4,64,1024]{2,1,0:T(8,128)(2,1)S(1)} %bitcast.4), channel_id=1, source_target_pairs={{32,0},{40,8},{48,16},{56,24},{64,32},{72,40},{80,48},{88,56},{96,... | collective-permute-start | bytes 1572872 | tf_op jit(solution)/shard_map/ppermute | solution.py:31
  15.7 0.0 collective-permute-start.5
  15.7 9.8 %collective-permute-done.refs_1_ = bf16[4,64,1024]{2,1,0:T(8,128)(2,1)S(1)} collective-permute-done((bf16[4,64,1024]{2,1,0:T(8,128)(2,1)S(1)}, bf16[4,64,1024]{2,1,0:T(8,128)(2,1)S(1)}, u32[]{:S(2)}, u32[]{:S(2)}) %collective-permute-start) | collective-permute-done | bytes 524320 | tf_op jit(solution)/shard_map/ppermute | solution.py:31
  25.5 0.1 collective-permute-start.2
  25.6 0.0 collective-permute-done.1.refs_2_
  25.6 3.3 %collective-permute-start.3 = (bf16[2,64,1024]{2,1,0:T(8,128)(2,1)S(1)}, bf16[2,64,1024]{2,1,0:T(8,128)(2,1)}, u32[]{:S(2)}, u32[]{:S(2)}) collective-permute-start(bf16[2,64,1024]{2,1,0:T(8,128)(2,1)S(1)} %slice.29), channel_id=1, source_target_pairs={{24,0},{0,8},{8,16},{16,24},{56,32},{32,40},{40,48},{48,56},{88,64... | collective-permute-start | bytes 786440 | tf_op jit(solution)/shard_map/ppermute | solution.py:31
  28.9 0.9 collective-permute-done.4.refs_6_
  29.9 3.7 %collective-permute-start.6 = (bf16[2,64,1024]{2,1,0:T(8,128)(2,1)S(1)}, bf16[2,64,1024]{2,1,0:T(8,128)(2,1)}, u32[]{:S(2)}, u32[]{:S(2)}) collective-permute-start(bf16[2,64,1024]{2,1,0:T(8,128)(2,1)S(1)} %slice.30), channel_id=1, source_target_pairs={{32,0},{40,8},{48,16},{56,24},{64,32},{72,40},{80,48},{88,56},{96,... | collective-permute-start | bytes 786440 | tf_op jit(solution)/shard_map/ppermute | solution.py:31
  33.6 2.1 %collective-permute-done.5.refs_7_ = bf16[4,64,1024]{2,1,0:T(8,128)(2,1)S(1)} collective-permute-done((bf16[4,64,1024]{2,1,0:T(8,128)(2,1)S(1)}, bf16[4,64,1024]{2,1,0:T(8,128)(2,1)S(1)}, u32[]{:S(2)}, u32[]{:S(2)}) %collective-permute-start.5) | collective-permute-done | bytes 524320 | tf_op jit(solution)/shard_map/ppermute | solution.py:31
  35.8 0.1 collective-permute-start.7
  35.9 0.6 slice.21
  36.5 1.3 fusion
  37.8 1.9 %pad_add_fusion.meta_ref.refs_0_ = s32[2]{0:T(128)} fusion(s32[1]{0:T(128)} %bitcast.1, s32[1]{0:T(128)} %slice.21), kind=kLoop, calls=%fused_computation.5 | loop fusion | flops 2 | bytes 16 | tf_op jit(solution)/shard_map/stack | solution.py:462
  39.6 0.0 copy-done.1
  39.7 0.0 collective-permute-done.2.refs_3_
  39.7 0.0 copy-start.14
  39.7 0.0 collective-permute-done.3.refs_4_
  39.7 0.8 collective-permute-done.6.refs_8_
  40.5 3.4 %collective-permute-done.7.refs_9_ = bf16[2,64,1024]{2,1,0:T(8,128)(2,1)} collective-permute-done((bf16[2,64,1024]{2,1,0:T(8,128)(2,1)S(1)}, bf16[2,64,1024]{2,1,0:T(8,128)(2,1)}, u32[]{:S(2)}, u32[]{:S(2)}) %collective-permute-start.7) | collective-permute-done | bytes 262176 | tf_op jit(solution)/shard_map/ppermute | solution.py:31
  44.0 3.8 %pick_items.1 = (bf16[2,64,1024]{2,1,0:T(8,128)(2,1)}, bf16[2,64,1024]{2,1,0:T(8,128)(2,1)}, bf16[2,64,1024]{2,1,0:T(8,128)(2,1)}, bf16[2,64,1024]{2,1,0:T(8,128...) custom-call(s32[2]{0:T(128)} %pad_add_fusion.meta_ref.refs_0_, ...), custom_call_target="tpu_custom_call" | custom-call | tf_op jit(solution)/shard_map/pick_items/pallas_call | solution.py:90
  47.8 0.1 collective-permute-start.10
  47.9 0.1 collective-permute-start.11
  47.9 1.7 %collective-permute-start.12 = (bf16[2,64,1024]{2,1,0:T(8,128)(2,1)}, bf16[2,64,1024]{2,1,0:T(8,128)(2,1)S(1)}, u32[]{:S(2)}, u32[]{:S(2)}) collective-permute-start(bf16[2,64,1024]{2,1,0:T(8,128)(2,1)} %get-tuple-element.21), channel_id=1, source_target_pairs={{16,0},{24,8},{0,16},{8,24},{48,32},{56,40},{32,48},{40,56},{80,64... | collective-permute-start | bytes 786440 | tf_op jit(solution)/shard_map/ppermute | solution.py:31
  49.7 1.5 %collective-permute-start.13 = (bf16[2,64,1024]{2,1,0:T(8,128)(2,1)}, bf16[2,64,1024]{2,1,0:T(8,128)(2,1)S(1)}, u32[]{:S(2)}, u32[]{:S(2)}) collective-permute-start(bf16[2,64,1024]{2,1,0:T(8,128)(2,1)} %get-tuple-element.22), channel_id=1, source_target_pairs={{24,0},{0,8},{8,16},{16,24},{56,32},{32,40},{40,48},{48,56},{88,64... | collective-permute-start | bytes 786440 | tf_op jit(solution)/shard_map/ppermute | solution.py:31
  51.2 3.2 %collective-permute-start.8 = (bf16[2,64,1024]{2,1,0:T(8,128)(2,1)}, bf16[2,64,1024]{2,1,0:T(8,128)(2,1)S(1)}, u32[]{:S(2)}, u32[]{:S(2)}) collective-permute-start(bf16[2,64,1024]{2,1,0:T(8,128)(2,1)} %get-tuple-element.16), channel_id=1, source_target_pairs={{32,0},{40,8},{48,16},{56,24},{64,32},{72,40},{80,48},{88,56},{96,... | collective-permute-start | bytes 786440 | tf_op jit(solution)/shard_map/ppermute | solution.py:31
  54.3 7.9 %collective-permute-done.10.refs_3_.refs_7_ = bf16[2,64,1024]{2,1,0:T(8,128)(2,1)S(1)} collective-permute-done((bf16[2,64,1024]{2,1,0:T(8,128)(2,1)}, bf16[2,64,1024]{2,1,0:T(8,128)(2,1)S(1)}, u32[]{:S(2)}, u32[]{:S(2)}) %collective-permute-start.10) | collective-permute-done | bytes 262176 | tf_op jit(solution)/shard_map/ppermute | solution.py:31
  62.2 0.0 collective-permute-start.9
  63.0 4.4 %collective-permute-done.11.refs_5_.refs_9_ = bf16[2,64,1024]{2,1,0:T(8,128)(2,1)S(1)} collective-permute-done((bf16[2,64,1024]{2,1,0:T(8,128)(2,1)}, bf16[2,64,1024]{2,1,0:T(8,128)(2,1)S(1)}, u32[]{:S(2)}, u32[]{:S(2)}) %collective-permute-start.11) | collective-permute-done | bytes 262176 | tf_op jit(solution)/shard_map/ppermute | solution.py:31
  67.3 3.7 %collective-permute-done.12.refs_6_.refs_10_ = bf16[2,64,1024]{2,1,0:T(8,128)(2,1)S(1)} collective-permute-done((bf16[2,64,1024]{2,1,0:T(8,128)(2,1)}, bf16[2,64,1024]{2,1,0:T(8,128)(2,1)S(1)}, u32[]{:S(2)}, u32[]{:S(2)}) %collective-permute-start.12) | collective-permute-done | bytes 262176 | tf_op jit(solution)/shard_map/ppermute | solution.py:31
  71.1 3.9 %collective-permute-done.13.refs_7_.refs_11_ = bf16[2,64,1024]{2,1,0:T(8,128)(2,1)S(1)} collective-permute-done((bf16[2,64,1024]{2,1,0:T(8,128)(2,1)}, bf16[2,64,1024]{2,1,0:T(8,128)(2,1)S(1)}, u32[]{:S(2)}, u32[]{:S(2)}) %collective-permute-start.13) | collective-permute-done | bytes 262176 | tf_op jit(solution)/shard_map/ppermute | solution.py:31
  75.0 0.0 collective-permute-done.8.refs_1_.refs_5_
  75.0 0.9 collective-permute-done.9.refs_2_.refs_6_
  75.9 0.0 copy-done.10
  75.9 0.0 copy-done.11
  75.9 0.7 copy-done.12
  76.6 3.0 %rank_part.1 = bf16[128,128]{1,0:T(8,128)(2,1)} custom-call(s32[2]{0:T(128)} %pad_add_fusion.meta_ref.refs_0_, s32[64]{0:T(128)} %slot_ref.5, s32[17]{0:T(128)} %segment_ref.5, bf16[256,1024]{1,0:T(8,128)(2,1)} %tokens_ref.1, bf16[2,64,1024]{2,1,0:T(8,128)(2,1)} %get-tuple-element.15.refs_0_.refs_4_, bf16[2,64,1024]{2,1,0:T(8,128)(2,1)} %copy-done.11, ...), custom_call_target="tpu_custom_call" | custom-call | tf_op jit(solution)/shard_map/rank_part/pallas_call | solution.py:158
  79.6 0.0 collective-permute-start.14
  79.6 0.1 maximum_maximum_fusion.refs_2_
  79.8 1.2 collective-permute-done.14
  81.0 4.2 %collective-permute-start.18 = (bf16[528,128]{1,0:T(8,128)(2,1)S(1)}, bf16[528,128]{1,0:T(8,128)(2,1)S(1)}, u32[]{:S(2)}, u32[]{:S(2)}) collective-permute-start(bf16[528,128]{1,0:T(8,128)(2,1)S(1)} %maximum_maximum_fusion.refs_2_), channel_id=1, source_target_pairs={{0,8},{8,16},{16,24},{24,32},{32,40},{40,48},{48,56},{56,64},{64,7... | collective-permute-start | bytes 405512 | tf_op jit(solution)/shard_map/ppermute | solution.py:485
  85.3 0.8 add_convert_fusion.refs_0_
  86.0 0.0 copy-start.16
  86.0 4.5 %collective-permute-start.15 = (bf16[128,128]{1,0:T(8,128)(2,1)S(1)}, bf16[128,128]{1,0:T(8,128)(2,1)S(1)}, u32[]{:S(2)}, u32[]{:S(2)}) collective-permute-start(bf16[128,128]{1,0:T(8,128)(2,1)S(1)} %add_convert_fusion.refs_0_), channel_id=1, source_target_pairs={{2,0},{3,1},{4,2},{5,3},{6,4},{7,5},{0,6},{1,7},{10,8},{11,9},{12,... | collective-permute-start | bytes 98312 | tf_op jit(solution)/shard_map/ppermute | solution.py:39
  90.6 0.0 collective-permute-start.16
  90.6 1.0 collective-permute-start.17
  91.6 0.6 collective-permute-done.15.refs_1_
  92.2 3.9 %collective-permute-done.16.refs_2_ = bf16[128,128]{1,0:T(8,128)(2,1)S(1)} collective-permute-done((bf16[128,128]{1,0:T(8,128)(2,1)S(1)}, bf16[128,128]{1,0:T(8,128)(2,1)S(1)}, u32[]{:S(2)}, u32[]{:S(2)}) %collective-permute-start.16) | collective-permute-done | bytes 32800 | tf_op jit(solution)/shard_map/ppermute | solution.py:39
  96.1 0.0 collective-permute-done.17.refs_3_
  96.1 0.6 copy-done.20
  96.7 0.6 copy-done.21
  97.3 3.3 %queries.1.refs_1_ = bf16[2560,128]{1,0:T(8,128)(2,1)} custom-call(s32[2]{0:T(128)} %pad_add_fusion.meta_ref.refs_0_, s32[64]{0:T(128)} %slot_ref.5, s32[17]{0:T(128)} %segment_ref.5, bf16[256,1024]{1,0:T(8,128)(2,1)} %base_ref.1, bf16[128,128]{1,0:T(8,128)(2,1)} %copy-done.16, bf16[128,128]{1,0:T(8,128)(2,1)} %copy-done.19, bf16[128,128]{1,0:T(8,128)(2,1)} %copy-done.20, ...), custom_call_target="tpu_custom_call" | custom-call | tf_op jit(solution)/shard_map/queries/pallas_call | solution.py:213
  100.5 0.0 collective-permute-done.18.refs_3_
  100.5 0.0 all-gather.2.cloned.1.call-done.refs_4_
  100.6 0.6 copy-done.15
  101.2 35.4 %attend.1 = bf16[256,1024]{1,0:T(8,128)(2,1)} custom-call(s32[2]{0:T(128)} %pad_add_fusion.meta_ref.refs_0_, bf16[2560,128]{1,0:T(8,128)(2,1)} %queries.1.refs_1_, bf16[528,128]{1,0:T(8,128)(2,1)} %copy-done.13, bf16[528,128]{1,0:T(8,128)(2,1)} %copy-done.15, bf16[33024,128]{1,0:T(8,128)(2,1)} %all-gather.2.cloned.1.call-done.refs_4_), custom_call_target="tpu_custom_call" | custom-call | tf_op jit(solution)/shard_map/attend/pallas_call | solution.py:421
  (43 shorter events, 0.2 us)
Async XLA Ops:
  6.5 2.7 %copy-start.6 = (bf16[4,2,64,1024]{3,2,1,0:T(8,128)(2,1)S(1)}, bf16[4,2,64,1024]{3,2,1,0:T(8,128)(2,1)}, u32[]{:S(2)}) copy-start(bf16[4,2,64,1024]{3,2,1,0:T(8,128)(2,1)} %param.17) | copy-start | bytes 3145732
  6.5 94.0 %all-gather.2.cloned.1.call-start = ((), (), s32[]{:S(2)}) async-start(), calls=%async_computation | async-start | bytes 8982528 | tf_op jit(solution)/shard_map/all_gather | solution.py:469
  9.3 30.3 %copy-start = (bf16[4,2,32,1024]{3,2,1,0:T(8,128)(2,1)}, bf16[4,2,32,1024]{3,2,1,0:T(8,128)(2,1)S(1)}, u32[]{:S(2)}) copy-start(bf16[4,2,32,1024]{3,2,1,0:T(8,128)(2,1)S(1)} %get-tuple-element.25) | copy-start | bytes 1572868
  9.3 30.3 %copy-start.1 = (bf16[4,2,32,1024]{3,2,1,0:T(8,128)(2,1)}, bf16[4,2,32,1024]{3,2,1,0:T(8,128)(2,1)S(1)}, u32[]{:S(2)}) copy-start(bf16[4,2,32,1024]{3,2,1,0:T(8,128)(2,1)S(1)} %get-tuple-element.26) | copy-start | bytes 1572868
  9.3 26.5 %copy-start.22 = (s32[256]{0:T(256)S(1)}, s32[256]{0:T(256)}, u32[]{:S(2)}) copy-start(s32[256]{0:T(256)} %param.20) | copy-start | bytes 3076
  9.4 16.1 %collective-permute-start = (bf16[4,64,1024]{2,1,0:T(8,128)(2,1)S(1)}, bf16[4,64,1024]{2,1,0:T(8,128)(2,1)S(1)}, u32[]{:S(2)}, u32[]{:S(2)}) collective-permute-start(bf16[4,64,1024]{2,1,0:T(8,128)(2,1)S(1)} %bitcast.7), channel_id=1, source_target_pairs={{8,0},{16,8},{24,16},{0,24},{40,32},{48,40},{56,48},{32,56},{72,64... | collective-permute-start | bytes 1572872 | tf_op jit(solution)/shard_map/ppermute | solution.py:31
  10.2 15.3 %collective-permute-start.1 = (bf16[4,64,1024]{2,1,0:T(8,128)(2,1)S(1)}, bf16[4,64,1024]{2,1,0:T(8,128)(2,1)S(1)}, u32[]{:S(2)}, u32[]{:S(2)}) collective-permute-start(bf16[4,64,1024]{2,1,0:T(8,128)(2,1)S(1)} %bitcast.8), channel_id=1, source_target_pairs={{24,0},{0,8},{8,16},{16,24},{56,32},{32,40},{40,48},{48,56},{88,64... | collective-permute-start | bytes 1572872 | tf_op jit(solution)/shard_map/ppermute | solution.py:31
  12.7 17.2 %collective-permute-start.4 = (bf16[4,64,1024]{2,1,0:T(8,128)(2,1)S(1)}, bf16[4,64,1024]{2,1,0:T(8,128)(2,1)S(1)}, u32[]{:S(2)}, u32[]{:S(2)}) collective-permute-start(bf16[4,64,1024]{2,1,0:T(8,128)(2,1)S(1)} %bitcast.4), channel_id=1, source_target_pairs={{32,0},{40,8},{48,16},{56,24},{64,32},{72,40},{80,48},{88,56},{96,... | collective-permute-start | bytes 1572872 | tf_op jit(solution)/shard_map/ppermute | solution.py:31
  15.7 20.1 %collective-permute-start.5 = (bf16[4,64,1024]{2,1,0:T(8,128)(2,1)S(1)}, bf16[4,64,1024]{2,1,0:T(8,128)(2,1)S(1)}, u32[]{:S(2)}, u32[]{:S(2)}) collective-permute-start(bf16[4,64,1024]{2,1,0:T(8,128)(2,1)S(1)} %bitcast.5), channel_id=1, source_target_pairs={{96,0},{104,8},{112,16},{120,24},{0,32},{8,40},{16,48},{24,56},{32... | collective-permute-start | bytes 1572872 | tf_op jit(solution)/shard_map/ppermute | solution.py:31
  25.5 18.4 %copy-start.2 = (bf16[4,64,1024]{2,1,0:T(8,128)(2,1)}, bf16[4,64,1024]{2,1,0:T(8,128)(2,1)S(1)}, u32[]{:S(2)}) copy-start(bf16[4,64,1024]{2,1,0:T(8,128)(2,1)S(1)} %collective-permute-done.refs_1_) | copy-start | bytes 1572868
  25.5 14.2 %collective-permute-start.2 = (bf16[2,64,1024]{2,1,0:T(8,128)(2,1)S(1)}, bf16[2,64,1024]{2,1,0:T(8,128)(2,1)S(1)}, u32[]{:S(2)}, u32[]{:S(2)}) collective-permute-start(bf16[2,64,1024]{2,1,0:T(8,128)(2,1)S(1)} %slice.28), channel_id=1, source_target_pairs={{8,0},{16,8},{24,16},{0,24},{40,32},{48,40},{56,48},{32,56},{72,64... | collective-permute-start | bytes 786440 | tf_op jit(solution)/shard_map/ppermute | solution.py:31
  25.6 18.3 %copy-start.3 = (bf16[4,64,1024]{2,1,0:T(8,128)(2,1)}, bf16[4,64,1024]{2,1,0:T(8,128)(2,1)S(1)}, u32[]{:S(2)}) copy-start(bf16[4,64,1024]{2,1,0:T(8,128)(2,1)S(1)} %collective-permute-done.1.refs_2_) | copy-start | bytes 1572868
  25.6 14.0 %collective-permute-start.3 = (bf16[2,64,1024]{2,1,0:T(8,128)(2,1)S(1)}, bf16[2,64,1024]{2,1,0:T(8,128)(2,1)}, u32[]{:S(2)}, u32[]{:S(2)}) collective-permute-start(bf16[2,64,1024]{2,1,0:T(8,128)(2,1)S(1)} %slice.29), channel_id=1, source_target_pairs={{24,0},{0,8},{8,16},{16,24},{56,32},{32,40},{40,48},{48,56},{88,64... | collective-permute-start | bytes 786440 | tf_op jit(solution)/shard_map/ppermute | solution.py:31
  29.9 14.1 %copy-start.4 = (bf16[4,64,1024]{2,1,0:T(8,128)(2,1)}, bf16[4,64,1024]{2,1,0:T(8,128)(2,1)S(1)}, u32[]{:S(2)}) copy-start(bf16[4,64,1024]{2,1,0:T(8,128)(2,1)S(1)} %collective-permute-done.4.refs_6_) | copy-start | bytes 1572868
  29.9 10.6 %collective-permute-start.6 = (bf16[2,64,1024]{2,1,0:T(8,128)(2,1)S(1)}, bf16[2,64,1024]{2,1,0:T(8,128)(2,1)}, u32[]{:S(2)}, u32[]{:S(2)}) collective-permute-start(bf16[2,64,1024]{2,1,0:T(8,128)(2,1)S(1)} %slice.30), channel_id=1, source_target_pairs={{32,0},{40,8},{48,16},{56,24},{64,32},{72,40},{80,48},{88,56},{96,... | collective-permute-start | bytes 786440 | tf_op jit(solution)/shard_map/ppermute | solution.py:31
  35.7 8.2 %copy-start.5 = (bf16[4,64,1024]{2,1,0:T(8,128)(2,1)}, bf16[4,64,1024]{2,1,0:T(8,128)(2,1)S(1)}, u32[]{:S(2)}) copy-start(bf16[4,64,1024]{2,1,0:T(8,128)(2,1)S(1)} %collective-permute-done.5.refs_7_) | copy-start | bytes 1572868
  35.8 8.2 %collective-permute-start.7 = (bf16[2,64,1024]{2,1,0:T(8,128)(2,1)S(1)}, bf16[2,64,1024]{2,1,0:T(8,128)(2,1)}, u32[]{:S(2)}, u32[]{:S(2)}) collective-permute-start(bf16[2,64,1024]{2,1,0:T(8,128)(2,1)S(1)} %slice.31), channel_id=1, source_target_pairs={{96,0},{104,8},{112,16},{120,24},{0,32},{8,40},{16,48},{24,56},{32... | collective-permute-start | bytes 786440 | tf_op jit(solution)/shard_map/ppermute | solution.py:31
  39.7 4.3 %copy-start.14 = (bf16[2,64,1024]{2,1,0:T(8,128)(2,1)}, bf16[2,64,1024]{2,1,0:T(8,128)(2,1)S(1)}, u32[]{:S(2)}) copy-start(bf16[2,64,1024]{2,1,0:T(8,128)(2,1)S(1)} %collective-permute-done.2.refs_3_) | copy-start | bytes 786436
  47.8 14.4 %collective-permute-start.10 = (bf16[2,64,1024]{2,1,0:T(8,128)(2,1)}, bf16[2,64,1024]{2,1,0:T(8,128)(2,1)S(1)}, u32[]{:S(2)}, u32[]{:S(2)}) collective-permute-start(bf16[2,64,1024]{2,1,0:T(8,128)(2,1)} %get-tuple-element.18), channel_id=1, source_target_pairs={{96,0},{104,8},{112,16},{120,24},{0,32},{8,40},{16,48},{24,56},{32... | collective-permute-start | bytes 786440 | tf_op jit(solution)/shard_map/ppermute | solution.py:31
  47.9 19.5 %collective-permute-start.11 = (bf16[2,64,1024]{2,1,0:T(8,128)(2,1)}, bf16[2,64,1024]{2,1,0:T(8,128)(2,1)S(1)}, u32[]{:S(2)}, u32[]{:S(2)}) collective-permute-start(bf16[2,64,1024]{2,1,0:T(8,128)(2,1)} %get-tuple-element.20), channel_id=1, source_target_pairs={{8,0},{16,8},{24,16},{0,24},{40,32},{48,40},{56,48},{32,56},{72,64... | collective-permute-start | bytes 786440 | tf_op jit(solution)/shard_map/ppermute | solution.py:31
  47.9 23.1 %collective-permute-start.12 = (bf16[2,64,1024]{2,1,0:T(8,128)(2,1)}, bf16[2,64,1024]{2,1,0:T(8,128)(2,1)S(1)}, u32[]{:S(2)}, u32[]{:S(2)}) collective-permute-start(bf16[2,64,1024]{2,1,0:T(8,128)(2,1)} %get-tuple-element.21), channel_id=1, source_target_pairs={{16,0},{24,8},{0,16},{8,24},{48,32},{56,40},{32,48},{40,56},{80,64... | collective-permute-start | bytes 786440 | tf_op jit(solution)/shard_map/ppermute | solution.py:31
  49.7 25.3 %collective-permute-start.13 = (bf16[2,64,1024]{2,1,0:T(8,128)(2,1)}, bf16[2,64,1024]{2,1,0:T(8,128)(2,1)S(1)}, u32[]{:S(2)}, u32[]{:S(2)}) collective-permute-start(bf16[2,64,1024]{2,1,0:T(8,128)(2,1)} %get-tuple-element.22), channel_id=1, source_target_pairs={{24,0},{0,8},{8,16},{16,24},{56,32},{32,40},{40,48},{48,56},{88,64... | collective-permute-start | bytes 786440 | tf_op jit(solution)/shard_map/ppermute | solution.py:31
  51.2 23.8 %collective-permute-start.8 = (bf16[2,64,1024]{2,1,0:T(8,128)(2,1)}, bf16[2,64,1024]{2,1,0:T(8,128)(2,1)S(1)}, u32[]{:S(2)}, u32[]{:S(2)}) collective-permute-start(bf16[2,64,1024]{2,1,0:T(8,128)(2,1)} %get-tuple-element.16), channel_id=1, source_target_pairs={{32,0},{40,8},{48,16},{56,24},{64,32},{72,40},{80,48},{88,56},{96,... | collective-permute-start | bytes 786440 | tf_op jit(solution)/shard_map/ppermute | solution.py:31
  62.2 13.7 %copy-start.7 = (bf16[2,64,1024]{2,1,0:T(8,128)(2,1)}, bf16[2,64,1024]{2,1,0:T(8,128)(2,1)S(1)}, u32[]{:S(2)}) copy-start(bf16[2,64,1024]{2,1,0:T(8,128)(2,1)S(1)} %collective-permute-done.10.refs_3_.refs_7_) | copy-start | bytes 786436
  62.2 13.7 %collective-permute-start.9 = (bf16[2,64,1024]{2,1,0:T(8,128)(2,1)}, bf16[2,64,1024]{2,1,0:T(8,128)(2,1)S(1)}, u32[]{:S(2)}, u32[]{:S(2)}) collective-permute-start(bf16[2,64,1024]{2,1,0:T(8,128)(2,1)} %get-tuple-element.17), channel_id=1, source_target_pairs={{64,0},{72,8},{80,16},{88,24},{96,32},{104,40},{112,48},{120,56},{... | collective-permute-start | bytes 786440 | tf_op jit(solution)/shard_map/ppermute | solution.py:31
  67.3 8.6 %copy-start.8 = (bf16[2,64,1024]{2,1,0:T(8,128)(2,1)}, bf16[2,64,1024]{2,1,0:T(8,128)(2,1)S(1)}, u32[]{:S(2)}) copy-start(bf16[2,64,1024]{2,1,0:T(8,128)(2,1)S(1)} %collective-permute-done.11.refs_5_.refs_9_) | copy-start | bytes 786436
  71.1 4.8 %copy-start.9 = (bf16[2,64,1024]{2,1,0:T(8,128)(2,1)}, bf16[2,64,1024]{2,1,0:T(8,128)(2,1)S(1)}, u32[]{:S(2)}) copy-start(bf16[2,64,1024]{2,1,0:T(8,128)(2,1)S(1)} %collective-permute-done.12.refs_6_.refs_10_) | copy-start | bytes 786436
  75.0 0.9 copy-start.10
  75.0 0.9 copy-start.11
  75.9 0.7 copy-start.12
  76.6 3.0 %copy-start.17 = (bf16[256,128]{1,0:T(8,128)(2,1)S(1)}, bf16[256,128]{1,0:T(8,128)(2,1)}, u32[]{:S(2)}) copy-start(bf16[256,128]{1,0:T(8,128)(2,1)} %param.14) | copy-start | bytes 196612
  76.6 3.0 %copy-start.18 = (bf16[256,128]{1,0:T(8,128)(2,1)S(1)}, bf16[256,128]{1,0:T(8,128)(2,1)}, u32[]{:S(2)}) copy-start(bf16[256,128]{1,0:T(8,128)(2,1)} %param.13) | copy-start | bytes 196612
  79.6 1.4 collective-permute-start.14
  79.8 20.7 %copy-start.13 = (bf16[528,128]{1,0:T(8,128)(2,1)}, bf16[528,128]{1,0:T(8,128)(2,1)S(1)}, u32[]{:S(2)}) copy-start(bf16[528,128]{1,0:T(8,128)(2,1)S(1)} %maximum_maximum_fusion.refs_2_) | copy-start | bytes 405508
  81.0 19.5 %collective-permute-start.18 = (bf16[528,128]{1,0:T(8,128)(2,1)S(1)}, bf16[528,128]{1,0:T(8,128)(2,1)S(1)}, u32[]{:S(2)}, u32[]{:S(2)}) collective-permute-start(bf16[528,128]{1,0:T(8,128)(2,1)S(1)} %maximum_maximum_fusion.refs_2_), channel_id=1, source_target_pairs={{0,8},{8,16},{16,24},{24,32},{32,40},{40,48},{48,56},{56,64},{64,7... | collective-permute-start | bytes 405512 | tf_op jit(solution)/shard_map/ppermute | solution.py:485
  86.0 10.0 %copy-start.16 = (bf16[128,128]{1,0:T(8,128)(2,1)}, bf16[128,128]{1,0:T(8,128)(2,1)S(1)}, u32[]{:S(2)}) copy-start(bf16[128,128]{1,0:T(8,128)(2,1)S(1)} %add_convert_fusion.refs_0_) | copy-start | bytes 98308
  86.0 6.1 %collective-permute-start.15 = (bf16[128,128]{1,0:T(8,128)(2,1)S(1)}, bf16[128,128]{1,0:T(8,128)(2,1)S(1)}, u32[]{:S(2)}, u32[]{:S(2)}) collective-permute-start(bf16[128,128]{1,0:T(8,128)(2,1)S(1)} %add_convert_fusion.refs_0_), channel_id=1, source_target_pairs={{2,0},{3,1},{4,2},{5,3},{6,4},{7,5},{0,6},{1,7},{10,8},{11,9},{12,... | collective-permute-start | bytes 98312 | tf_op jit(solution)/shard_map/ppermute | solution.py:39
  90.6 5.5 %collective-permute-start.16 = (bf16[128,128]{1,0:T(8,128)(2,1)S(1)}, bf16[128,128]{1,0:T(8,128)(2,1)S(1)}, u32[]{:S(2)}, u32[]{:S(2)}) collective-permute-start(bf16[128,128]{1,0:T(8,128)(2,1)S(1)} %add_convert_fusion.refs_0_), channel_id=1, source_target_pairs={{4,0},{5,1},{6,2},{7,3},{0,4},{1,5},{2,6},{3,7},{12,8},{13,9},{14,... | collective-permute-start | bytes 98312 | tf_op jit(solution)/shard_map/ppermute | solution.py:39
  90.6 5.5 %collective-permute-start.17 = (bf16[128,128]{1,0:T(8,128)(2,1)S(1)}, bf16[128,128]{1,0:T(8,128)(2,1)S(1)}, u32[]{:S(2)}, u32[]{:S(2)}) collective-permute-start(bf16[128,128]{1,0:T(8,128)(2,1)S(1)} %add_convert_fusion.refs_0_), channel_id=1, source_target_pairs={{6,0},{7,1},{0,2},{1,3},{2,4},{3,5},{4,6},{5,7},{14,8},{15,9},{8,1... | collective-permute-start | bytes 98312 | tf_op jit(solution)/shard_map/ppermute | solution.py:39
  92.2 3.9 %copy-start.19 = (bf16[128,128]{1,0:T(8,128)(2,1)}, bf16[128,128]{1,0:T(8,128)(2,1)S(1)}, u32[]{:S(2)}) copy-start(bf16[128,128]{1,0:T(8,128)(2,1)S(1)} %collective-permute-done.15.refs_1_) | copy-start | bytes 98308
  96.0 0.6 copy-start.20
  96.6 0.6 copy-start.21
  100.5 0.6 copy-start.15
Sparse Core Ops, SparseCore 0:
  9.6 89.0 all-gather.1
